TPU v7x, 256 devices: a whole 4x4x8 slice. The times are simulated.
256 devices in a mesh: dp: 16 (over z_hi, y, core), mp: 16 (over x, z_lo).
Axes of the slice: x: 4, y: 4, z: 8 (z_hi: 2, z_lo: 4; z = z_hi * 4 + z_lo), core: 2. Of those that a mesh axis runs over, the one named last changes fastest.
Arguments:
- student_rows: bfloat16 [12288, 256], P('dp'), may hold values from -12 to 12
- teacher_rows: bfloat16 [12288, 256], P('dp'), may hold values from -12 to 12
- student_protos: bfloat16 [256, 131072], P(None, 'mp'), may hold values from -12 to 12
- teacher_protos: bfloat16 [256, 131072], P(None, 'mp'), may hold values from -12 to 12
- center: float32 [131072], P('mp'), may hold values from -0.25 to 0.25
- row_weight: float32 [12288], P('dp'), may hold values from 0.25 to 4
Outputs:
- grad_rows: float32 [12288, 256], P('dp')
- proto_grad: float32 [256, 131072], P('dp', 'mp')
All inputs are finite; a program needn't handle non-finite values.
Results may differ from a plain program's by a relative error of at most 0.012.
The roundings to bfloat16 on the way count: a program that leaves them out, or rounds other values in their place, can miss the bound.
Values sent between devices are 32-bit elements; how exact they have to be, the bound alone decides.
No kernel may reach another device: no remote copies, remote signals or barrier semaphores. Data moves between devices by JAX's collectives and lax.ppermute only.
A program may use at most 192 MiB of HBM per device.

v0:
```python
import jax
import jax.numpy as jnp
from jax import lax
from jax.sharding import PartitionSpec as P

student_temp = 0.1
teacher_temp = 0.04
norm_eps = 1e-06


def local(student_rows, teacher_rows, student_protos, teacher_protos, center, row_weight):
    s_full = student_rows.astype(jnp.float32)
    row_norm = jnp.sqrt(jnp.sum(s_full * s_full, axis=1, keepdims=True) + norm_eps)
    z_unit = s_full / row_norm
    z_student = z_unit.astype(jnp.bfloat16)
    t_full = teacher_rows.astype(jnp.float32)
    z_teacher = (
        t_full / jnp.sqrt(jnp.sum(t_full * t_full, axis=1, keepdims=True) + norm_eps)
    ).astype(jnp.bfloat16)
    v_full = student_protos.astype(jnp.float32)
    col_norm = jnp.sqrt(jnp.sum(v_full * v_full, axis=0, keepdims=True) + norm_eps)
    w_student = (v_full / col_norm).astype(jnp.bfloat16)
    u_full = teacher_protos.astype(jnp.float32)
    w_teacher = (
        u_full / jnp.sqrt(jnp.sum(u_full * u_full, axis=0, keepdims=True) + norm_eps)
    ).astype(jnp.bfloat16)
    s_logit = jnp.dot(z_student, w_student, preferred_element_type=jnp.float32)
    t_logit = jnp.dot(z_teacher, w_teacher, preferred_element_type=jnp.float32)
    e_student = jnp.exp((s_logit - 1.0) / student_temp)
    e_teacher = jnp.exp((t_logit - center[None, :] - 1.0) / teacher_temp)
    sum_student, sum_teacher = lax.psum(
        (jnp.sum(e_student, axis=1), jnp.sum(e_teacher, axis=1)), "mp"
    )
    grad_logit = (
        row_weight[:, None]
        * (e_student / sum_student[:, None] - e_teacher / sum_teacher[:, None])
        / student_temp
    ).astype(jnp.bfloat16)
    partial_value = lax.dot_general(
        grad_logit, w_student, (((1,), (1,)), ((), ())), preferred_element_type=jnp.float32
    )
    grad_unit = lax.psum(partial_value, "mp")
    grad_rows = (grad_unit - z_unit * jnp.sum(z_unit * grad_unit, axis=1, keepdims=True)) / row_norm
    features = student_rows.shape[1]
    feature_rows = features // lax.axis_size("dp")
    grad_w = lax.psum_scatter(
        lax.dot_general(
            z_student, grad_logit, (((0,), (0,)), ((), ())), preferred_element_type=jnp.float32
        ),
        "dp",
        scatter_dimension=0,
        tiled=True,
    )
    w_mine = lax.dynamic_slice_in_dim(
        w_student, lax.axis_index("dp") * feature_rows, feature_rows, 0
    ).astype(jnp.float32)
    col_dot = lax.psum(jnp.sum(w_mine * grad_w, axis=0), "dp")
    proto_grad = (grad_w - w_mine * col_dot[None, :]) / col_norm
    return (grad_rows, proto_grad)


def solution(mesh):
    placed = (P("dp", None), P("dp", None), P(None, "mp"), P(None, "mp"), P("mp"), P("dp"))
    return jax.shard_map(
        local, mesh=mesh, in_specs=placed, out_specs=(P("dp", None), P("dp", "mp")), check_vma=False
    )
```

profile of v0, /device:TPU:32, one launch (start us, length us, event | category | flops | bytes accessed | tf_op | source)
XLA Modules:
  0.0 415.5 jit_solution(17623355280237728845)
XLA Ops:
  8.0 0.0 copy-start.1
  8.0 0.0 copy-start.5
  8.0 0.0 all-reduce.3.cloned.1.call-start
  8.1 0.0 copy-start.4
  8.1 3.2 fusion.2
  11.3 3.2 fusion.3
  14.5 0.0 copy-done.1
  14.5 0.0 copy-start.2
  14.5 0.2 fusion.9
  14.7 0.0 copy-done.4
  14.7 0.9 fusion.4
  15.6 0.0 copy-done.5
  15.6 0.2 fusion.10
  15.8 0.7 copy-done.2
  16.5 0.0 copy-start.6
  16.5 11.1 %fusion = (f32[768]{0:T(1024)S(1)}, f32[768,8192]{1,0:T(8,128)}) fusion(bf16[256,8192]{1,0:T(8,128)(2,1)S(1)} %fusion.3, f32[768]{0:T(1024)S(1)} %add_sqrt_fusion.3, bf16[768,256]{1,0:T(8,128)(2,1)S(1)} %copy-done.1), kind=kOutput, calls=%fused_computation.3 | convolution fusion | flops 3240688896 | bytes 29759488 | tf_op jit(solution)/shard_map/dot_general | solution.py:27
  27.7 0.0 copy-done.6
  27.7 0.0 copy-start.7
  27.7 11.4 %fusion.1 = (f32[768]{0:T(1024)S(1)}, f32[768,8192]{1,0:T(8,128)}) fusion(f32[8192]{0:T(1024)S(1)} %copy-done.6, bf16[256,8192]{1,0:T(8,128)(2,1)S(1)} %copy-done.4, f32[8192]{0:T(1024)S(1)} %add_sqrt_fusion, bf16[768,256]{1,0:T(8,128)(2,1)S(1)} %copy-done.5, f32[768]{0:T(1024)S(1)} %add_sqrt_fusion.2), kind=kOutput, calls=%fused_computation.4 | convolution fusion | flops 3253271808 | bytes 29825024 | tf_op jit(solution)/shard_map/dot_general | solution.py:28
  39.0 40.6 %all-reduce = (f32[768]{0:T(1024)S(1)}, f32[768]{0:T(1024)S(1)}) all-reduce(f32[768]{0:T(1024)S(1)} %get-tuple-element.4, f32[768]{0:T(1024)S(1)} %get-tuple-element.6), channel_id=1, replica_groups=mesh['dp'=16,'mp'=16] {'mp'}, use_global_device_ids=true, to_apply=%region_7.0 | all-reduce | flops 1536 | bytes 12288 | tf_op jit(solution)/shard_map/psum | solution.py:31
  79.6 0.0 copy-done.7
  79.6 0.0 copy-start.3
  79.6 19.7 %multiply_convert_fusion = bf16[768,8192]{1,0:T(8,128)(2,1)S(1)} fusion(f32[768,8192]{1,0:T(8,128)} %get-tuple-element.7, f32[768,8192]{1,0:T(8,128)} %get-tuple-element.5, f32[768]{0:T(1024)S(1)} %get-tuple-element.2, f32[8192]{0:T(1024)S(1)} %copy-done.6, f32[768]{0:T(1024)S(1)} %get-tuple-element.3, f32[768]{0:T(1024)S(1)} %copy-done.7), kind=kLoop, calls=%fused_computation | loop fusion | flops 69206016 | bytes 62956544 | tf_op jit(solution)/shard_map/convert_element_type | solution.py:38
  99.3 0.0 copy-start
  99.3 4.6 %copy-done = bf16[768,8192]{1,0:T(8,128)(2,1)} copy-done((bf16[768,8192]{1,0:T(8,128)(2,1)}, bf16[768,8192]{1,0:T(8,128)(2,1)S(1)}, u32[]{:S(2)}) %copy-start) | copy-done | bytes 12582936
  103.9 0.0 copy-done.3
  103.9 4.3 %fusion.21 = f32[768,256]{1,0:T(8,128)} fusion(bf16[768,8192]{1,0:T(8,128)(2,1)S(1)} %multiply_convert_fusion, bf16[256,8192]{1,0:T(8,128)(2,1)S(1)} %copy-done.3), kind=kOutput, calls=%fused_computation.38 | convolution fusion | flops 3221225472 | bytes 17563648 | tf_op jit(solution)/shard_map/dot_general | solution.py:39
  108.2 0.0 all-reduce.3.cloned.1.call-update
  108.3 0.0 reduce-scatter.2.cloned.1.call-start
  108.3 10.5 %fusion.17 = f32[256,8192]{1,0:T(8,128)} fusion(bf16[768,8192]{1,0:T(8,128)(2,1)} %copy-done, bf16[768,256]{1,0:T(8,128)(2,1)S(1)} %copy-done.1, f32[768]{0:T(1024)S(1)} %add_sqrt_fusion.3), kind=kOutput, calls=%fused_computation.30 | convolution fusion | flops 3221815296 | bytes 21367808 | tf_op jit(solution)/shard_map/dot_general | solution.py:47
  118.8 0.0 reduce-scatter.2.cloned.1.call-update
  118.8 198.1 %all-reduce.3.cloned.1.call-done = f32[768,256]{1,0:T(8,128)} async-done(((f32[768,256]{1,0:T(8,128)}), f32[768,256]{1,0:T(8,128)}) %all-reduce.3.cloned.1.call-update) | async-done | bytes 786448 | tf_op jit(solution)/shard_map/psum | solution.py:42
  317.0 1.4 multiply_reduce_fusion
  318.4 2.3 subtract_divide_fusion
  320.7 0.0 reduce-scatter.2.cloned.1.call-done
  320.7 1.2 fusion.12
  321.9 84.2 %psum.31 = f32[8192]{0:T(1024)S(1)} all-reduce(f32[8192]{0:T(1024)S(1)} %fusion.12), channel_id=1, replica_groups=mesh['dp'=16,'mp'=16] {'dp'}, use_global_device_ids=true, to_apply=%region_12.0 | all-reduce | flops 8192 | bytes 65536 | tf_op jit(solution)/shard_map/psum | solution.py:57
  406.1 2.0 fusion.14
  (4 shorter events, 0.0 us)
Async XLA Ops:
  8.0 6.5 %copy-start.1 = (bf16[768,256]{1,0:T(8,128)(2,1)S(1)}, bf16[768,256]{1,0:T(8,128)(2,1)}, u32[]{:S(2)}) copy-start(bf16[768,256]{1,0:T(8,128)(2,1)} %param.6) | copy-start | bytes 1179652
  8.0 7.6 %copy-start.5 = (bf16[768,256]{1,0:T(8,128)(2,1)S(1)}, bf16[768,256]{1,0:T(8,128)(2,1)}, u32[]{:S(2)}) copy-start(bf16[768,256]{1,0:T(8,128)(2,1)} %param.7) | copy-start | bytes 1179652
  8.0 308.9 %all-reduce.3.cloned.1.call-start = ((), (), s32[]{:S(2)}) async-start(), calls=%async_computation.1 | async-start | bytes 1572864 | tf_op jit(solution)/shard_map/psum | solution.py:42
  8.1 6.6 %copy-start.4 = (bf16[256,8192]{1,0:T(8,128)(2,1)S(1)}, bf16[256,8192]{1,0:T(8,128)(2,1)}, u32[]{:S(2)}) copy-start(bf16[256,8192]{1,0:T(8,128)(2,1)} %param.9) | copy-start | bytes 12582916
  14.5 2.0 copy-start.2
  16.5 11.1 %copy-start.6 = (f32[8192]{0:T(1024)S(1)}, f32[8192]{0:T(1024)}, u32[]{:S(2)}) copy-start(f32[8192]{0:T(1024)} %param.10) | copy-start | bytes 98308
  27.7 51.9 %copy-start.7 = (f32[768]{0:T(1024)S(1)}, f32[768]{0:T(1024)}, u32[]{:S(2)}) copy-start(f32[768]{0:T(1024)} %param.11) | copy-start | bytes 9220
  79.6 24.3 %copy-start.3 = (bf16[256,8192]{1,0:T(8,128)(2,1)S(1)}, bf16[256,8192]{1,0:T(8,128)(2,1)}, u32[]{:S(2)}) copy-start(bf16[256,8192]{1,0:T(8,128)(2,1)} %copy-done.2) | copy-start | bytes 12582916
  99.3 4.6 %copy-start = (bf16[768,8192]{1,0:T(8,128)(2,1)}, bf16[768,8192]{1,0:T(8,128)(2,1)S(1)}, u32[]{:S(2)}) copy-start(bf16[768,8192]{1,0:T(8,128)(2,1)S(1)} %multiply_convert_fusion) | copy-start | bytes 37748740
  108.3 212.4 %reduce-scatter.2.cloned.1.call-start = ((), (), s32[]{:S(2)}) async-start(), calls=%async_computation.2 | async-start | bytes 8912896 | tf_op jit(solution)/shard_map/reduce_scatter | solution.py:46
Sparse Core Ops, SparseCore 0:
  108.4 208.5 all-reduce.2
Sparse Core Ops, SparseCore 1:
  118.9 143.9 reduce-scatter.1
where the time goes:
time: 416 us; the launch traced here: 415 us
  waiting for transfers between devices  198 us (48%)
  blocking collectives  125 us (30%)
  matrix products  37.3 us (9%)
  other arithmetic  34.3 us (8%)
  between operations  15.7 us (4%)
  local copies, waits for them, and re-layouts  5.3 us (1%)
    psum x1, waiting for transfers between devices, local(): grad_unit = lax.psum(partial_value, 'mp')  198 us
    psum x1, blocking collectives, local(): col_dot = lax.psum(jnp.sum(w_mine * grad_w, axis=0), 'dp')  84.2 us
    psum x1, blocking collectives, local(): lax.psum((jnp.sum(e_student, axis=1), jnp.sum(e_teacher, axis=1)), 'mp')  40.6 us
    convert_element_type x1, other arithmetic, local(): grad_logit = (row_weight[:, None] * (e_student / sum_student[:, None] - e...  19.7 us
    dot_general x1, matrix products, local(): t_logit = jnp.dot(z_teacher, w_teacher, preferred_element_type=jnp.float32)  11.4 us
    dot_general x1, matrix products, local(): s_logit = jnp.dot(z_student, w_student, preferred_element_type=jnp.float32)  11.1 us
    dot_general x1, matrix products, local(): lax.dot_general(z_student, grad_logit, (((0,), (0,)), ((), ())), preferre...  10.5 us
  transfers between devices with their start and end apart: 2, of which 1 were waited for; matrix products, arithmetic and copies ran while one was open for 3% of the time, Pallas kernels for 0%

commit v1 on v0

v1 whole, which is shorter than its diff:
```python
import functools
import jax
import jax.numpy as jnp
import numpy as np
from jax import lax
from jax.experimental import pallas as pl
from jax.experimental.pallas import tpu as pltpu
from jax.sharding import PartitionSpec as P

student_temp = 0.1
teacher_temp = 0.04
norm_eps = 1e-06
LOG2E = 1.4426950408889634
F32 = jnp.float32
BF16 = jnp.bfloat16
TILE = 512
ROWBLK = 256
CHUNKS = (1024, 1536, 1536)
MIB = 1 << 20


def call(kernel, out, *args, vmem=40, flops=0, nbytes=0, **kw):
    return pl.pallas_call(
        kernel,
        out_shape=out,
        compiler_params=pltpu.CompilerParams(vmem_limit_bytes=vmem * MIB),
        cost_estimate=pl.CostEstimate(flops=flops, bytes_accessed=nbytes, transcendentals=0),
        **kw,
    )(*args)


def shape(dims, dtype=F32):
    return jax.ShapeDtypeStruct(dims, dtype)


def prep_kernel(s_ref, t_ref, z_ref):
    for i, ref in enumerate((s_ref, t_ref)):
        v = ref[...].astype(F32)
        z_ref[i] = v / jnp.sqrt(jnp.sum(v * v, axis=1, keepdims=True) + norm_eps)


def unit_columns(ref):
    v = ref[...].astype(F32)
    inv = 1.0 / jnp.sqrt(jnp.sum(v * v, axis=0, keepdims=True) + norm_eps)
    return (v * inv).astype(BF16), inv


def logits_pass(z_ref, w_s, w_t, center_ref, es_ref, et_ref, sums_ref, zb, acc, last):
    @pl.when(pl.program_id(0) == 0)
    def _():
        zb[...] = z_ref[...].astype(BF16)
        acc[...] = jnp.zeros_like(acc)

    shift = center_ref[...] * (LOG2E / teacher_temp)
    rows = zb.shape[1]
    for r in range(rows // ROWBLK):
        part = pl.ds(r * ROWBLK, ROWBLK)
        for i, (w, e_ref) in enumerate(((w_s, es_ref), (w_t, et_ref))):
            logit = jnp.dot(zb[i, part, :], w, preferred_element_type=F32)
            if i == 0:
                e = jnp.exp2(logit * (LOG2E / student_temp))
            else:
                e = jnp.exp2(logit * (LOG2E / teacher_temp) - shift)
            total = e[:, :128]
            for k in range(1, TILE // 128):
                total = total + e[:, k * 128 : (k + 1) * 128]
            acc[i, part, :] += total
            e_ref[part, :] = e.astype(BF16)

    @pl.when(pl.program_id(0) == last)
    def _():
        for i in range(2):
            sums_ref[i : i + 1, :] = jnp.sum(acc[i].T, axis=0, keepdims=True)


def own_kernel(last, core_ref, z_ref, sp_ref, tp_ref, center_ref,
               es_ref, et_ref, ws_ref, wt_ref, inv_ref, sums_ref, zb, acc):
    w_s, inv = unit_columns(sp_ref)
    w_t, _ = unit_columns(tp_ref)
    ws_ref[...] = w_s
    wt_ref[...] = w_t
    inv_ref[...] = inv
    logits_pass(z_ref, w_s, w_t, center_ref, es_ref, et_ref, sums_ref, zb, acc, last)


def other_kernel(last, core_ref, z_ref, ws_ref, wt_ref, center_ref, mine_ref, weight_ref,
                 es_ref, et_ref, pay_ref, zb, acc):
    logits_pass(z_ref, ws_ref[...], wt_ref[...], center_ref, es_ref, et_ref,
                pay_ref.at[2:4], zb, acc, last)

    @pl.when(pl.program_id(0) == 0)
    def _():
        pay_ref[0:2, :] = mine_ref[...]
        pay_ref[4:5, :] = weight_ref[...]
        pay_ref[5:8, :] = jnp.zeros_like(pay_ref[5:8, :])


def chip_kernel(mine_ref, theirs_ref, out_ref):
    out_ref[0:2, :] = mine_ref[0:2, :] + theirs_ref[2:4, :]
    out_ref[2:4, :] = mine_ref[2:4, :] + theirs_ref[0:2, :]
    out_ref[4:5, :] = mine_ref[4:5, :]
    out_ref[5:6, :] = theirs_ref[4:5, :]
    out_ref[6:8, :] = jnp.zeros_like(out_ref[6:8, :])


def add4_kernel(a_ref, b_ref, c_ref, d_ref, out_ref):
    out_ref[0:4, :] = a_ref[0:4, :] + b_ref[0:4, :] + c_ref[0:4, :] + d_ref[0:4, :]
    out_ref[4:8, :] = a_ref[4:8, :]


def factors_kernel(a_ref, b_ref, c_ref, d_ref, out_ref):
    total = a_ref[0:4, :] + b_ref[0:4, :] + c_ref[0:4, :] + d_ref[0:4, :]
    for i in range(4):
        weight = a_ref[4 + i // 2 : 5 + i // 2, :]
        f = weight / (total[i : i + 1, :] * student_temp)
        out_ref[i] = jnp.broadcast_to(f, (128, f.shape[1])).T


def unit_kernel(es_ref, et_ref, ws_ref, z_ref, perm_ref, u_ref, zt_ref):
    @pl.when(pl.program_id(0) == 0)
    def _():
        u_ref[...] = jnp.zeros_like(u_ref)
        zt_ref[...] = lax.dot_general(
            perm_ref[...], z_ref[0].astype(BF16), (((1,), (1,)), ((), ())), preferred_element_type=F32
        ).astype(BF16)

    w = ws_ref[...]
    for i, ref in enumerate((es_ref, et_ref)):
        u_ref[i] += lax.dot_general(
            ref[...], w, (((1,), (1,)), ((), ())), preferred_element_type=F32
        )


def combine_kernel(f_ref, u_ref, v_ref, own_ref, other_ref):
    for k in range(2):
        lanes = slice(k * 128, (k + 1) * 128)
        own_ref[:, lanes] = f_ref[0] * u_ref[0, :, lanes] - f_ref[1] * u_ref[1, :, lanes]
        other_ref[:, lanes] = f_ref[2] * v_ref[0, :, lanes] - f_ref[3] * v_ref[1, :, lanes]


def grad_kernel(blocks_ref, f_ref, eso_ref, eto_ref, esx_ref, etx_ref, zo_ref, zx_ref, ws_ref, inv_ref,
                own_ref, bp_ref, bm_ref, ap_ref, am_ref, g):
    for j, (s_ref, t_ref) in enumerate(((eso_ref, eto_ref), (esx_ref, etx_ref))):
        for k in range(TILE // 128):
            lanes = slice(k * 128, (k + 1) * 128)
            g[j, :, lanes] = (
                f_ref[2 * j] * s_ref[:, lanes].astype(F32)
                - f_ref[2 * j + 1] * t_ref[:, lanes].astype(F32)
            ).astype(BF16)
    grad = jnp.dot(zo_ref[...], g[0], preferred_element_type=F32)
    grad = grad + jnp.dot(zx_ref[...], g[1], preferred_element_type=F32)
    w = [ws_ref[pl.ds(pl.multiple_of(blocks_ref[i] * 16, 16), 16), :].astype(F32) for i in range(16)]
    dot = jnp.zeros((16, TILE), F32)
    for i in range(16):
        dot = dot + w[i] * grad[i * 16 : (i + 1) * 16]
    dot = jnp.sum(dot, axis=0, keepdims=True)
    inv = inv_ref[...]
    homes = (
        [(own_ref, i * 16) for i in range(4)]
        + [(bp_ref, i * 16) for i in range(4)]
        + [(bm_ref, i * 16) for i in range(4)]
        + [(ap_ref, 0), (ap_ref, 16), (am_ref, 0), (am_ref, 16)]
    )
    for i, (ref, at) in enumerate(homes):
        ref[at : at + 16, :] = (grad[i * 16 : (i + 1) * 16] - w[i] * dot) * inv


def ring_kernel(bp_ref, bm_ref, rp_ref, rm_ref, op_ref, om_ref):
    op_ref[0:32, :] = bp_ref[0:32, :] + rp_ref[...]
    op_ref[32:64, :] = bp_ref[32:64, :]
    om_ref[0:32, :] = bm_ref[0:32, :]
    om_ref[32:64, :] = bm_ref[32:64, :] + rm_ref[...]


def ring_end_kernel(own_ref, rp_ref, rm_ref, k_ref, c_ref, z_ref, zc_ref):
    for i, ref in enumerate((k_ref, c_ref, z_ref, zc_ref)):
        rows = slice(i * 16, (i + 1) * 16)
        ref[...] = own_ref[rows, :] + rp_ref[rows, :] + rm_ref[rows, :]


def protos_kernel(core_ref, *refs):
    out_ref = refs[-1]
    half = out_ref.shape[1] // 2
    mine = core_ref[0] * half
    theirs = (1 - core_ref[0]) * half
    at = 0
    for i, width in enumerate(CHUNKS):
        k_ref, c_ref, z_ref, zc_ref = refs[4 * i : 4 * i + 4]
        out_ref[:, pl.ds(pl.multiple_of(mine + at, 128), width)] = k_ref[...] + z_ref[...]
        out_ref[:, pl.ds(pl.multiple_of(theirs + at, 128), width)] = c_ref[...] + zc_ref[...]
        at += width


def split_kernel(x_ref, own_ref, got_ref, o0_ref, op_ref, om_ref, o2_ref):
    size = o0_ref.shape[0]
    for step, ref in ((0, o0_ref), (1, op_ref), (3, om_ref), (2, o2_ref)):
        rows = pl.ds(pl.multiple_of(lax.rem(x_ref[0] + step, 4) * size, 16), size)
        ref[...] = own_ref[rows, :] + got_ref[rows, :]


def sum4_kernel(a_ref, b_ref, c_ref, d_ref, out_ref):
    out_ref[...] = a_ref[...] + b_ref[...] + c_ref[...] + d_ref[...]


def rows_kernel(x_ref, a_ref, b_ref, c_ref, d_ref, rows_ref, out_ref):
    total = a_ref[...] + b_ref[...] + c_ref[...] + d_ref[...]
    size = out_ref.shape[0]
    v = rows_ref[pl.ds(pl.multiple_of(x_ref[0] * size, 16), size), :].astype(F32)
    norm = jnp.sqrt(jnp.sum(v * v, axis=1, keepdims=True) + norm_eps)
    z = v / norm
    out_ref[...] = (total - z * jnp.sum(z * total, axis=1, keepdims=True)) / norm


def place_kernel(x_ref, a_ref, p_ref, m_ref, t_ref, out_ref):
    size = a_ref.shape[0]
    for step, ref in ((0, a_ref), (3, p_ref), (1, m_ref), (2, t_ref)):
        rows = pl.ds(pl.multiple_of(lax.rem(x_ref[0] + step, 4) * size, 16), size)
        out_ref[rows, :] = ref[...]


def dp_pairs(move):
    def at(z, y, c):
        return (z * 4 + y) * 2 + c
    return [(at(z, y, c), at(*move(z, y, c))) for z in range(2) for y in range(4) for c in range(2)]


def mp_pairs(dx, dz):
    return [(x * 4 + z, (x + dx) % 4 * 4 + (z + dz) % 4) for x in range(4) for z in range(4)]


CORE = dp_pairs(lambda z, y, c: (z, y, 1 - c))
YP = dp_pairs(lambda z, y, c: (z, (y + 1) % 4, c))
YM = dp_pairs(lambda z, y, c: (z, (y - 1) % 4, c))
ZZ = dp_pairs(lambda z, y, c: (1 - z, y, c))
ZZC = dp_pairs(lambda z, y, c: (1 - z, y, 1 - c))


def to_dp(v, pairs):
    return lax.ppermute(v, "dp", pairs)


def to_mp(v, dx, dz):
    return lax.ppermute(v, "mp", mp_pairs(dx, dz))


def prefetch(grid, in_specs, out_specs, scratch=()):
    return pltpu.PrefetchScalarGridSpec(
        num_scalar_prefetch=1, grid=grid, in_specs=in_specs, out_specs=out_specs, scratch_shapes=scratch
    )


VM = pl.BlockSpec(memory_space=pltpu.VMEM)
SM = pl.BlockSpec(memory_space=pltpu.SMEM)


def local(student_rows, teacher_rows, student_protos, teacher_protos, center, row_weight):
    rows, feats = student_rows.shape
    protos = student_protos.shape[1]
    half = protos // 2
    dp = lax.axis_index("dp")
    core, y, z_hi = dp % 2, dp // 2 % 4, dp // 8
    x = lax.axis_index("mp") // 4
    core_s = core.astype(jnp.int32)[None]
    x_s = x.astype(jnp.int32)[None]
    blocks = jnp.stack([
        ((z_hi ^ zr) * 4 + (y + yr) % 4) * 2 + (core ^ cr)
        for yr in (0, 1, 3, 2) for zr in (0, 1) for cr in (0, 1)
    ]).astype(jnp.int32)
    source = jnp.repeat(blocks, 16) * 16 + jnp.arange(feats, dtype=jnp.int32) % 16
    perm = (source[:, None] == jnp.arange(feats, dtype=jnp.int32)[None, :]).astype(BF16)

    z = call(prep_kernel, shape((2, rows, feats)), student_rows, teacher_rows,
             in_specs=[VM, VM], out_specs=VM, nbytes=3 * MIB)
    z_other = to_dp(z, CORE)

    tiles = half // TILE
    center2 = center[None, :]
    weight2 = row_weight[None, :]
    z_spec = pl.BlockSpec((2, rows, feats), lambda i, c: (0, 0, 0))
    wide = lambda i, c: (0, c[0] * tiles + i)
    tile = lambda i, c: (0, i)
    fixed = lambda i, c: (0, 0)
    e_shape = shape((rows, half), BF16)
    e_spec = pl.BlockSpec((rows, TILE), tile)
    w_spec = pl.BlockSpec((feats, TILE), tile)
    pass_scratch = (pltpu.VMEM((2, rows, feats), BF16), pltpu.VMEM((2, rows, 128), F32))
    flops = 4 * rows * feats * half
    es_o, et_o, ws, wt, inv, sums = call(
        functools.partial(own_kernel, tiles - 1),
        (e_shape, e_shape, shape((feats, half), BF16), shape((feats, half), BF16), shape((1, half)), shape((2, rows))),
        core_s, z, student_protos, teacher_protos, center2,
        grid_spec=prefetch(
            (tiles,),
            [z_spec, pl.BlockSpec((feats, TILE), wide), pl.BlockSpec((feats, TILE), wide), pl.BlockSpec((1, TILE), wide)],
            [e_spec, e_spec, w_spec, w_spec, pl.BlockSpec((1, TILE), tile), pl.BlockSpec((2, rows), fixed)],
            pass_scratch,
        ),
        flops=flops, nbytes=20 * MIB,
    )
    es_x, et_x, pay = call(
        functools.partial(other_kernel, tiles - 1),
        (e_shape, e_shape, shape((8, rows))),
        core_s, z_other, ws, wt, center2, sums, weight2,
        grid_spec=prefetch(
            (tiles,),
            [z_spec, w_spec, w_spec, pl.BlockSpec((1, TILE), wide), pl.BlockSpec((2, rows), fixed), pl.BlockSpec((1, rows), fixed)],
            [e_spec, e_spec, pl.BlockSpec((8, rows), fixed)],
            pass_scratch,
        ),
        flops=flops, nbytes=20 * MIB,
    )
    small = dict(in_specs=[VM] * 2, out_specs=VM)
    small4 = dict(in_specs=[VM] * 4, out_specs=VM)
    tot = call(chip_kernel, shape((8, rows)), pay, to_dp(pay, CORE), **small)
    tot = call(add4_kernel, shape((8, rows)), tot, *[to_mp(tot, k, 0) for k in (1, 2, 3)], **small4)
    tot = [tot] + [to_mp(tot, 0, k) for k in (1, 2, 3)]

    def unit(es, et, zz):
        ut = 2 * TILE
        return call(
            unit_kernel, (shape((2, rows, feats)), shape((feats, rows), BF16)), es, et, ws, zz, perm,
            grid=(half // ut,),
            in_specs=[
                pl.BlockSpec((rows, ut), lambda i: (0, i)), pl.BlockSpec((rows, ut), lambda i: (0, i)),
                pl.BlockSpec((feats, ut), lambda i: (0, i)), pl.BlockSpec((1, rows, feats), lambda i: (0, 0, 0)),
                pl.BlockSpec((feats, feats), lambda i: (0, 0)),
            ],
            out_specs=[pl.BlockSpec((2, rows, feats), lambda i: (0, 0, 0)), pl.BlockSpec((feats, rows), lambda i: (0, 0))],
            flops=flops, nbytes=18 * MIB,
        )

    u_o, zt_o = unit(es_o, et_o, z)
    u_x, zt_x = unit(es_x, et_x, z_other)
    f = call(factors_kernel, shape((4, rows, 128)), *tot, **small4)

    def chunk(at, width):
        first = at // TILE
        t = lambda i, b: (0, first + i)
        o = lambda i, b: (0, i)
        e = pl.BlockSpec((rows, TILE), t)
        zt = pl.BlockSpec((feats, rows), lambda i, b: (0, 0))
        return call(
            grad_kernel, (*[shape((64, width))] * 3, *[shape((32, width))] * 2),
            blocks, f, es_o, et_o, es_x, et_x, zt_o, zt_x, ws, inv,
            grid_spec=prefetch(
                (width // TILE,),
                [pl.BlockSpec((4, rows, 128), lambda i, b: (0, 0, 0)), e, e, e, e, zt, zt,
                 pl.BlockSpec((feats, TILE), t), pl.BlockSpec((1, TILE), t)],
                [pl.BlockSpec((64, TILE), o)] * 3 + [pl.BlockSpec((32, TILE), o)] * 2,
                (pltpu.VMEM((2, rows, TILE), BF16),),
            ),
            flops=flops * width // half, nbytes=26 * MIB * width // half,
        )

    parts = []
    at = 0
    for width in CHUNKS:
        own, bp, bm, ap, am = chunk(at, width)
        bp, bm = call(ring_kernel, (shape((64, width)),) * 2, bp, bm, to_dp(ap, YP), to_dp(am, YM),
                      in_specs=[VM] * 4, out_specs=[VM] * 2, input_output_aliases={0: 0, 1: 1})
        keep, c, zz, zc = call(ring_end_kernel, (shape((16, width)),) * 4, own, to_dp(bp, YP), to_dp(bm, YM),
                               in_specs=[VM] * 3, out_specs=[VM] * 4)
        parts += [keep, to_dp(c, CORE), to_dp(zz, ZZ), to_dp(zc, ZZC)]
        at += width

    g_own, g_other = call(combine_kernel, (shape((rows, feats)),) * 2, f, u_o, u_x,
                          in_specs=[VM] * 3, out_specs=[VM] * 2)
    quarter = shape((rows // 4, feats))
    o0, op, om, o2 = call(split_kernel, (quarter,) * 4, x_s, g_own, to_dp(g_other, CORE),
                          in_specs=[SM, VM, VM], out_specs=[VM] * 4)
    part = call(sum4_kernel, quarter, o0, to_mp(op, 1, 0), to_mp(om, 3, 0), to_mp(o2, 2, 0), **small4)
    mine = call(rows_kernel, quarter, x_s, part, *[to_mp(part, 0, k) for k in (1, 2, 3)], student_rows,
                in_specs=[SM] + [VM] * 5, out_specs=VM)
    grad_rows = call(place_kernel, shape((rows, feats)), x_s, mine, to_mp(mine, 1, 0), to_mp(mine, 3, 0), to_mp(mine, 2, 0),
                     in_specs=[SM] + [VM] * 4, out_specs=VM)
    proto_grad = call(protos_kernel, shape((16, protos)), core_s, *parts,
                      in_specs=[SM] + [VM] * len(parts), out_specs=VM)
    return grad_rows, proto_grad


def solution(mesh):
    placed = (P("dp", None), P("dp", None), P(None, "mp"), P(None, "mp"), P("mp"), P("dp"))
    return jax.shard_map(
        local, mesh=mesh, in_specs=placed, out_specs=(P("dp", None), P("dp", "mp")), check_vma=False
    )
```

time: 416 us -> 177 us (0.43)
  the two profiles are of different devices: /device:TPU:32 before, /device:TPU:1 now
where the time goes in v1:
time: 177 us; the launch traced here: 176 us
  starting transfers between devices  74.1 us (42%)
  Pallas kernels  59.2 us (33%)
  waiting for transfers between devices  24.9 us (14%)
  local copies, waits for them, and re-layouts  16.4 us (9%)
    pallas_call x23, Pallas kernels, call(): pl.pallas_call(kernel, out_shape=out, compiler_params=pltpu.CompilerParam...  59.2 us
    ppermute x24, starting transfers between devices, to_dp(): return lax.ppermute(v, 'dp', pairs)  57.1 us
    ppermute x15, starting transfers between devices, to_mp(): return lax.ppermute(v, 'mp', mp_pairs(dx, dz))  17.1 us
    unnamed x52, local copies, waits for them, and re-layouts  16.2 us
    ppermute x15, waiting for transfers between devices, to_mp(): return lax.ppermute(v, 'mp', mp_pairs(dx, dz))  13.5 us
    ppermute x24, waiting for transfers between devices, to_dp(): return lax.ppermute(v, 'dp', pairs)  11.4 us
  transfers between devices with their start and end apart: 39, of which 7 were waited for; matrix products, arithmetic and copies ran while one was open for 0% of the time, Pallas kernels for 28%

profile of v1, /device:TPU:1, one launch (start us, length us, event | category | flops | bytes accessed | tf_op | source)
XLA Modules:
  0.0 175.8 jit_solution(5687361661617088185)
XLA Ops:
  0.6 1.0 copy-done.7
  1.6 1.0 copy-done.12
  3.1 3.3 %collective-permute-start = (f32[2,768,256]{2,1,0:T(8,128)S(1)}, f32[2,768,256]{2,1,0:T(8,128)S(1)}, u32[]{:S(2)}, u32[]{:S(2)}) collective-permute-start(f32[2,768,256]{2,1,0:T(8,128)S(1)} %shard_map.77.z_ref), channel_id=1, source_target_pairs={{0,16},{16,0},{32,48},{48,32},{64,80},{80,64},{96,112},{112,96},{1... | collective-permute-start | bytes 4718600 | tf_op jit(solution)/shard_map/ppermute | solution.py:239
  6.7 2.2 %copy-done.20 = bf16[256,8192]{1,0:T(8,128)(2,1)S(1)} copy-done((bf16[256,8192]{1,0:T(8,128)(2,1)S(1)}, bf16[256,8192]{1,0:T(8,128)(2,1)}, u32[]{:S(2)}) %copy-start.20) | copy-done | bytes 4194328
  8.9 2.2 %copy-done.21 = bf16[256,8192]{1,0:T(8,128)(2,1)S(1)} copy-done((bf16[256,8192]{1,0:T(8,128)(2,1)S(1)}, bf16[256,8192]{1,0:T(8,128)(2,1)}, u32[]{:S(2)}) %copy-start.21) | copy-done | bytes 4194328
  11.1 9.6 %shard_map.78 = (bf16[768,4096]{1,0:T(8,128)(2,1)}, bf16[768,4096]{1,0:T(8,128)(2,1)}, bf16[256,4096]{1,0:T(8,128)(2,1)S(1)}, bf16[256,4096]{1,0:T(8,128)(2,1)S(...) custom-call(s32[1]{0:T(128)} %bitcast.1.core_ref, f32[2,768,256]{2,1,0:T(8,128)S(1)} %shard_map.77.z_ref, ...), custom_call_target="tpu_custom_call" | custom-call | flops 3221225472 | bytes 20971520 | tf_op jit(solution)/shard_map/pallas_call | solution.py:23
  20.7 1.1 copy-done.9
  21.9 1.6 copy-done.10
  23.4 7.9 %shard_map.79 = (bf16[768,4096]{1,0:T(8,128)(2,1)S(1)}, bf16[768,4096]{1,0:T(8,128)(2,1)}, f32[8,768]{1,0:T(8,128)S(1)}) custom-call(s32[1]{0:T(128)} %bitcast.1.core_ref, f32[2,768,256]{2,1,0:T(8,128)S(1)} %copy-done.10, bf16[256,4096]{1,0:T(8,128)(2,1)S(1)} %get-tuple-element.54.ws_ref, bf16[256,4096]{1,0:T(8,128)(2,1)S(1)} %get-tuple-element.55.wt_ref, ...), custom_call_target="tpu_custom_call" | custom-call | flops 3221225472 | bytes 20971520 | tf_op jit(solution)/shard_map/pallas_call | solution.py:23
  34.6 1.6 copy-done.2
  36.2 6.8 %shard_map.83 = (f32[2,768,256]{2,1,0:T(8,128)S(1)}, bf16[256,768]{1,0:T(8,128)(2,1)S(1)}) custom-call(bf16[768,4096]{1,0:T(8,128)(2,1)S(1)} %bitcast.20, bf16[768,4096]{1,0:T(8,128)(2,1)} %get-tuple-element.59.et_ref.eto_ref, bf16[256,4096]{1,0:T(8,128)(2,1)S(1)} %copy-done.2, f32[2,768,256]{2,1,0:T(8,128)S(1)} %copy-done.6, bf16[256,256]{1,0:T(8,128)(2,1)S(1)} %fusion.perm_ref), custom_call_target="tpu_custom_call" | custom-call | flops 3221225472 | bytes 18874368 | tf_op jit(solution)/shard_map/pallas_call | solution.py:23
  43.0 4.4 %collective-permute-start.7 = (f32[8,768]{1,0:T(8,128)S(1)}, f32[8,768]{1,0:T(8,128)S(1)}, u32[]{:S(2)}, u32[]{:S(2)}) collective-permute-start(f32[8,768]{1,0:T(8,128)S(1)} %shard_map.81.a_ref), channel_id=1, source_target_pairs={{0,3},{1,0},{2,1},{3,2},{4,7},{5,4},{6,5},{7,6},{8,11},{9,8},{10,9... | collective-permute-start | bytes 73736 | tf_op jit(solution)/shard_map/ppermute | solution.py:243
  47.8 1.4 copy-done.11
  49.2 6.7 %shard_map.84 = (f32[2,768,256]{2,1,0:T(8,128)S(1)}, bf16[256,768]{1,0:T(8,128)(2,1)S(1)}) custom-call(bf16[768,4096]{1,0:T(8,128)(2,1)S(1)} %get-tuple-element.61.es_ref.esx_ref, bf16[768,4096]{1,0:T(8,128)(2,1)} %get-tuple-element.62.et_ref.etx_ref, bf16[256,4096]{1,0:T(8,128)(2,1)S(1)} %copy-done.3, f32[2,768,256]{2,1,0:T(8,128)S(1)} %copy-done.11, ...), custom_call_target="tpu_custom_call" | custom-call | flops 3221225472 | bytes 18874368 | tf_op jit(solution)/shard_map/pallas_call | solution.py:23
  56.8 1.8 %collective-permute-start.8 = (f32[768,256]{1,0:T(8,128)S(1)}, f32[768,256]{1,0:T(8,128)S(1)}, u32[]{:S(2)}, u32[]{:S(2)}) collective-permute-start(f32[768,256]{1,0:T(8,128)S(1)} %get-tuple-element.65), channel_id=1, source_target_pairs={{0,16},{16,0},{32,48},{48,32},{64,80},{80,64},{96,112},{112,96},{1... | collective-permute-start | bytes 2359304 | tf_op jit(solution)/shard_map/ppermute | solution.py:239
  58.6 5.4 %shard_map.90 = (f32[64,1024]{1,0:T(8,128)S(1)}, f32[64,1024]{1,0:T(8,128)}, f32[64,1024]{1,0:T(8,128)}, f32[32,1024]{1,0:T(8,128)S(1)}, f32[32,1024]{1,0:T(8,128)S(1)}) custom-call(s32[16]{0:T(128)S(1)} %stack.67.blocks_ref, f32[4,768,128]{2,1,0:T(8,128)S(1)} %shard_map.82.f_ref, bf16[768,4096]{1,0:T(8,128)(2,1)S(1)} %bitcast.20, ...), custom_call_target="tpu_custom_call" | custom-call | flops 805306368 | bytes 6815744 | tf_op jit(solution)/shard_map/pallas_call | solution.py:23
  64.0 1.3 collective-permute-start.18
  65.3 1.5 collective-permute-start.19
  66.8 7.1 %shard_map.93 = (f32[64,1536]{1,0:T(8,128)S(1)}, f32[64,1536]{1,0:T(8,128)S(1)}, f32[64,1536]{1,0:T(8,128)S(1)}, f32[32,1536]{1,0:T(8,128)S(1)}, f32[32,1536]{1,0:T(8,128)}) custom-call(s32[16]{0:T(128)S(1)} %stack.67.blocks_ref, f32[4,768,128]{2,1,0:T(8,128)S(1)} %shard_map.82.f_ref, bf16[768,4096]{1,0:T(8,128)(2,1)S(1)} %bitcast.20, ...), custom_call_target="tpu_custom_call" | custom-call | flops 1207959552 | bytes 10223616 | tf_op jit(solution)/shard_map/pallas_call | solution.py:23
  74.7 1.8 %shard_map.91 = (f32[64,1024]{1,0:T(8,128)}, f32[64,1024]{1,0:T(8,128)}) custom-call(f32[64,1024]{1,0:T(8,128)} %get-tuple-element.74.bp_ref, f32[64,1024]{1,0:T(8,128)} %get-tuple-element.75.bm_ref, f32[32,1024]{1,0:T(8,128)S(1)} %collective-permute-done.18.rp_ref, ...), custom_call_target="tpu_custom_call", output_to_operand_aliasing={{0}: (0, {}), {1}: (1, {})} | custom-call | tf_op jit(solution)/shard_map/pallas_call | solution.py:23
  76.5 1.2 collective-permute-start.20
  77.7 1.4 collective-permute-start.26
  79.2 1.5 collective-permute-start.21
  80.6 7.1 %shard_map.96 = (f32[64,1536]{1,0:T(8,128)S(1)}, f32[64,1536]{1,0:T(8,128)S(1)}, f32[64,1536]{1,0:T(8,128)S(1)}, f32[32,1536]{1,0:T(8,128)}, f32[32,1536]{1,0:T(8,128)}) custom-call(s32[16]{0:T(128)S(1)} %stack.67.blocks_ref, f32[4,768,128]{2,1,0:T(8,128)S(1)} %shard_map.82.f_ref, bf16[768,4096]{1,0:T(8,128)(2,1)S(1)} %bitcast.20, ...), custom_call_target="tpu_custom_call" | custom-call | flops 1207959552 | bytes 10223616 | tf_op jit(solution)/shard_map/pallas_call | solution.py:23
  88.4 2.7 %collective-permute-start.33 = (f32[32,1536]{1,0:T(8,128)}, f32[32,1536]{1,0:T(8,128)}, u32[]{:S(2)}, u32[]{:S(2)}) collective-permute-start(f32[32,1536]{1,0:T(8,128)} %get-tuple-element.99), channel_id=1, source_target_pairs={{0,96},{16,112},{32,0},{48,16},{64,32},{80,48},{96,64},{112,80},{1... | collective-permute-start | bytes 589832 | tf_op jit(solution)/shard_map/ppermute | solution.py:239
  91.1 1.6 collective-permute-start.9
  92.7 1.2 collective-permute-start.10
  93.9 1.0 copy-done.14
  95.8 1.0 shard_map.94
  97.6 1.1 shard_map.92
  98.7 3.0 %collective-permute-start.28 = (f32[64,1536]{1,0:T(8,128)}, f32[64,1536]{1,0:T(8,128)S(1)}, u32[]{:S(2)}, u32[]{:S(2)}) collective-permute-start(f32[64,1536]{1,0:T(8,128)} %copy-done.15), channel_id=1, source_target_pairs={{0,96},{16,112},{32,0},{48,16},{64,32},{80,48},{96,64},{112,80},{1... | collective-permute-start | bytes 1179656 | tf_op jit(solution)/shard_map/ppermute | solution.py:239
  101.7 4.2 %collective-permute-start.22 = (f32[16,1024]{1,0:T(8,128)S(1)}, f32[16,1024]{1,0:T(8,128)S(1)}, u32[]{:S(2)}, u32[]{:S(2)}) collective-permute-start(f32[16,1024]{1,0:T(8,128)S(1)} %get-tuple-element.81), channel_id=1, source_target_pairs={{0,16},{16,0},{32,48},{48,32},{64,80},{80,64},{96,112},{112,96},{1... | collective-permute-start | bytes 196616 | tf_op jit(solution)/shard_map/ppermute | solution.py:239
  107.3 1.2 shard_map.97
  108.6 2.7 %collective-permute-start.35 = (f32[64,1536]{1,0:T(8,128)S(1)}, f32[64,1536]{1,0:T(8,128)S(1)}, u32[]{:S(2)}, u32[]{:S(2)}) collective-permute-start(f32[64,1536]{1,0:T(8,128)S(1)} %get-tuple-element.101), channel_id=1, source_target_pairs={{0,96},{16,112},{32,0},{48,16},{64,32},{80,48},{96,64},{112,80},{1... | collective-permute-start | bytes 1179656 | tf_op jit(solution)/shard_map/ppermute | solution.py:239
  111.2 3.2 %collective-permute-done.11.d_ref = f32[192,256]{1,0:T(8,128)S(1)} collective-permute-done((f32[192,256]{1,0:T(8,128)S(1)}, f32[192,256]{1,0:T(8,128)S(1)}, u32[]{:S(2)}, u32[]{:S(2)}) %collective-permute-start.11) | collective-permute-done | bytes 196640 | tf_op jit(solution)/shard_map/ppermute | solution.py:243
  114.4 5.1 %collective-permute-start.23 = (f32[16,1024]{1,0:T(8,128)S(1)}, f32[16,1024]{1,0:T(8,128)S(1)}, u32[]{:S(2)}, u32[]{:S(2)}) collective-permute-start(f32[16,1024]{1,0:T(8,128)S(1)} %get-tuple-element.82), channel_id=1, source_target_pairs={{0,128},{16,144},{32,160},{48,176},{64,192},{80,208},{96,224},{112... | collective-permute-start | bytes 196616 | tf_op jit(solution)/shard_map/ppermute | solution.py:239
  119.6 2.0 %collective-permute-done.23.refs_2_ = f32[16,1024]{1,0:T(8,128)S(1)} collective-permute-done((f32[16,1024]{1,0:T(8,128)S(1)}, f32[16,1024]{1,0:T(8,128)S(1)}, u32[]{:S(2)}, u32[]{:S(2)}) %collective-permute-start.23) | collective-permute-done | bytes 65568 | tf_op jit(solution)/shard_map/ppermute | solution.py:239
  121.6 2.9 %collective-permute-start.14 = (f32[192,256]{1,0:T(8,128)S(1)}, f32[192,256]{1,0:T(8,128)S(1)}, u32[]{:S(2)}, u32[]{:S(2)}) collective-permute-start(f32[192,256]{1,0:T(8,128)S(1)} %shard_map.87.a_ref), channel_id=1, source_target_pairs={{0,3},{1,0},{2,1},{3,2},{4,7},{5,4},{6,5},{7,6},{8,11},{9,8},{10,9... | collective-permute-start | bytes 589832 | tf_op jit(solution)/shard_map/ppermute | solution.py:243
  124.4 1.5 collective-permute-start.13
  126.0 3.0 %collective-permute-start.29 = (f32[16,1536]{1,0:T(8,128)S(1)}, f32[16,1536]{1,0:T(8,128)S(1)}, u32[]{:S(2)}, u32[]{:S(2)}) collective-permute-start(f32[16,1536]{1,0:T(8,128)S(1)} %get-tuple-element.92), channel_id=1, source_target_pairs={{0,16},{16,0},{32,48},{48,32},{64,80},{80,64},{96,112},{112,96},{1... | collective-permute-start | bytes 294920 | tf_op jit(solution)/shard_map/ppermute | solution.py:239
  129.0 4.0 %collective-permute-start.30 = (f32[16,1536]{1,0:T(8,128)S(1)}, f32[16,1536]{1,0:T(8,128)S(1)}, u32[]{:S(2)}, u32[]{:S(2)}) collective-permute-start(f32[16,1536]{1,0:T(8,128)S(1)} %get-tuple-element.93), channel_id=1, source_target_pairs={{0,128},{16,144},{32,160},{48,176},{64,192},{80,208},{96,224},{112... | collective-permute-start | bytes 294920 | tf_op jit(solution)/shard_map/ppermute | solution.py:239
  132.9 4.5 %collective-permute-start.24 = (f32[16,1024]{1,0:T(8,128)S(1)}, f32[16,1024]{1,0:T(8,128)S(1)}, u32[]{:S(2)}, u32[]{:S(2)}) collective-permute-start(f32[16,1024]{1,0:T(8,128)S(1)} %get-tuple-element.83), channel_id=1, source_target_pairs={{0,144},{16,128},{32,176},{48,160},{64,208},{80,192},{96,240},{112... | collective-permute-start | bytes 196616 | tf_op jit(solution)/shard_map/ppermute | solution.py:239
  137.5 10.2 %collective-permute-done.13.c_ref = f32[192,256]{1,0:T(8,128)S(1)} collective-permute-done((f32[192,256]{1,0:T(8,128)S(1)}, f32[192,256]{1,0:T(8,128)S(1)}, u32[]{:S(2)}, u32[]{:S(2)}) %collective-permute-start.13) | collective-permute-done | bytes 196640 | tf_op jit(solution)/shard_map/ppermute | solution.py:243
  147.7 7.0 %collective-permute-start.31 = (f32[16,1536]{1,0:T(8,128)S(1)}, f32[16,1536]{1,0:T(8,128)S(1)}, u32[]{:S(2)}, u32[]{:S(2)}) collective-permute-start(f32[16,1536]{1,0:T(8,128)S(1)} %get-tuple-element.94), channel_id=1, source_target_pairs={{0,144},{16,128},{32,176},{48,160},{64,208},{80,192},{96,240},{112... | collective-permute-start | bytes 294920 | tf_op jit(solution)/shard_map/ppermute | solution.py:239
  155.5 2.3 %collective-permute-start.16 = (f32[192,256]{1,0:T(8,128)S(1)}, f32[192,256]{1,0:T(8,128)S(1)}, u32[]{:S(2)}, u32[]{:S(2)}) collective-permute-start(f32[192,256]{1,0:T(8,128)S(1)} %shard_map.88.a_ref), channel_id=1, source_target_pairs={{0,12},{1,13},{2,14},{3,15},{4,0},{5,1},{6,2},{7,3},{8,4},{9,5},{1... | collective-permute-start | bytes 589832 | tf_op jit(solution)/shard_map/ppermute | solution.py:243
  157.8 1.6 collective-permute-start.37
  159.5 7.0 %collective-permute-start.38 = (f32[16,1536]{1,0:T(8,128)S(1)}, f32[16,1536]{1,0:T(8,128)S(1)}, u32[]{:S(2)}, u32[]{:S(2)}) collective-permute-start(f32[16,1536]{1,0:T(8,128)S(1)} %get-tuple-element.105), channel_id=1, source_target_pairs={{0,144},{16,128},{32,176},{48,160},{64,208},{80,192},{96,240},{112... | collective-permute-start | bytes 294920 | tf_op jit(solution)/shard_map/ppermute | solution.py:239
  166.5 7.5 %collective-permute-done.38.refs_11_ = f32[16,1536]{1,0:T(8,128)S(1)} collective-permute-done((f32[16,1536]{1,0:T(8,128)S(1)}, f32[16,1536]{1,0:T(8,128)S(1)}, u32[]{:S(2)}, u32[]{:S(2)}) %collective-permute-start.38) | collective-permute-done | bytes 98336 | tf_op jit(solution)/shard_map/ppermute | solution.py:239
  (113 shorter events, 12.6 us)
Async XLA Ops:
  3.1 17.6 %copy-start.5 = (f32[2,768,256]{2,1,0:T(8,128)}, f32[2,768,256]{2,1,0:T(8,128)S(1)}, u32[]{:S(2)}) copy-start(f32[2,768,256]{2,1,0:T(8,128)S(1)} %shard_map.77.z_ref) | copy-start | bytes 4718596
  3.1 17.6 %collective-permute-start = (f32[2,768,256]{2,1,0:T(8,128)S(1)}, f32[2,768,256]{2,1,0:T(8,128)S(1)}, u32[]{:S(2)}, u32[]{:S(2)}) collective-permute-start(f32[2,768,256]{2,1,0:T(8,128)S(1)} %shard_map.77.z_ref), channel_id=1, source_target_pairs={{0,16},{16,0},{32,48},{48,32},{64,80},{80,64},{96,112},{112,96},{1... | collective-permute-start | bytes 4718600 | tf_op jit(solution)/shard_map/ppermute | solution.py:239
  20.7 10.7 %copy-start.1 = (bf16[256,4096]{1,0:T(8,128)(2,1)}, bf16[256,4096]{1,0:T(8,128)(2,1)S(1)}, u32[]{:S(2)}) copy-start(bf16[256,4096]{1,0:T(8,128)(2,1)S(1)} %get-tuple-element.54.ws_ref) | copy-start | bytes 6291460
  21.9 12.7 %slice-start = ((s8[6291456]{0:T(1024)(128)(4,1)}), s8[4194304]{0:T(1024)(128)(4,1)S(1)}, s32[]{:S(2)}) async-start(s8[6291456]{0:T(1024)(128)(4,1)} %bitcast.19), calls=%async_computation | async-start | bytes 8388608
  23.4 11.1 %slice-start.1 = ((s8[6291456]{0:T(1024)(128)(4,1)}), s8[2097152]{0:T(1024)(128)(4,1)S(1)}, s32[]{:S(2)}) async-start(s8[6291456]{0:T(1024)(128)(4,1)} %bitcast.19), calls=%async_computation.1 | async-start | bytes 4194304
  23.4 11.1 %copy-start.6 = (f32[2,768,256]{2,1,0:T(8,128)S(1)}, f32[2,768,256]{2,1,0:T(8,128)}, u32[]{:S(2)}) copy-start(f32[2,768,256]{2,1,0:T(8,128)} %copy-done.5) | copy-start | bytes 4718596
  31.4 16.4 %copy-start = (bf16[768,4096]{1,0:T(8,128)(2,1)}, bf16[768,4096]{1,0:T(8,128)(2,1)S(1)}, u32[]{:S(2)}) copy-start(bf16[768,4096]{1,0:T(8,128)(2,1)S(1)} %get-tuple-element.61.es_ref.esx_ref) | copy-start | bytes 18874372
  31.4 1.2 collective-permute-start.1
  32.6 10.4 %collective-permute-start.4 = (f32[8,768]{1,0:T(8,128)S(1)}, f32[8,768]{1,0:T(8,128)S(1)}, u32[]{:S(2)}, u32[]{:S(2)}) collective-permute-start(f32[8,768]{1,0:T(8,128)S(1)} %shard_map.80.a_ref), channel_id=1, source_target_pairs={{0,12},{1,13},{2,14},{3,15},{4,0},{5,1},{6,2},{7,3},{8,4},{9,5},{1... | collective-permute-start | bytes 73736 | tf_op jit(solution)/shard_map/ppermute | solution.py:243
  33.4 9.6 %collective-permute-start.3 = (f32[8,768]{1,0:T(8,128)S(1)}, f32[8,768]{1,0:T(8,128)S(1)}, u32[]{:S(2)}, u32[]{:S(2)}) collective-permute-start(f32[8,768]{1,0:T(8,128)S(1)} %shard_map.80.a_ref), channel_id=1, source_target_pairs={{0,8},{1,9},{2,10},{3,11},{4,12},{5,13},{6,14},{7,15},{8,0},{9,1},... | collective-permute-start | bytes 73736 | tf_op jit(solution)/shard_map/ppermute | solution.py:243
  33.9 9.0 %collective-permute-start.2 = (f32[8,768]{1,0:T(8,128)S(1)}, f32[8,768]{1,0:T(8,128)S(1)}, u32[]{:S(2)}, u32[]{:S(2)}) collective-permute-start(f32[8,768]{1,0:T(8,128)S(1)} %shard_map.80.a_ref), channel_id=1, source_target_pairs={{0,4},{1,5},{2,6},{3,7},{4,8},{5,9},{6,10},{7,11},{8,12},{9,13},{1... | collective-permute-start | bytes 73736 | tf_op jit(solution)/shard_map/ppermute | solution.py:243
  36.1 11.7 %copy-start.3 = (bf16[256,4096]{1,0:T(8,128)(2,1)S(1)}, bf16[256,4096]{1,0:T(8,128)(2,1)}, u32[]{:S(2)}) copy-start(bf16[256,4096]{1,0:T(8,128)(2,1)} %copy-done.1) | copy-start | bytes 6291460
  43.0 12.9 %collective-permute-start.7 = (f32[8,768]{1,0:T(8,128)S(1)}, f32[8,768]{1,0:T(8,128)S(1)}, u32[]{:S(2)}, u32[]{:S(2)}) collective-permute-start(f32[8,768]{1,0:T(8,128)S(1)} %shard_map.81.a_ref), channel_id=1, source_target_pairs={{0,3},{1,0},{2,1},{3,2},{4,7},{5,4},{6,5},{7,6},{8,11},{9,8},{10,9... | collective-permute-start | bytes 73736 | tf_op jit(solution)/shard_map/ppermute | solution.py:243
  47.4 8.5 %collective-permute-start.6 = (f32[8,768]{1,0:T(8,128)S(1)}, f32[8,768]{1,0:T(8,128)S(1)}, u32[]{:S(2)}, u32[]{:S(2)}) collective-permute-start(f32[8,768]{1,0:T(8,128)S(1)} %shard_map.81.a_ref), channel_id=1, source_target_pairs={{0,2},{1,3},{2,0},{3,1},{4,6},{5,7},{6,4},{7,5},{8,10},{9,11},{10,... | collective-permute-start | bytes 73736 | tf_op jit(solution)/shard_map/ppermute | solution.py:243
  47.4 8.5 %collective-permute-start.5 = (f32[8,768]{1,0:T(8,128)S(1)}, f32[8,768]{1,0:T(8,128)S(1)}, u32[]{:S(2)}, u32[]{:S(2)}) collective-permute-start(f32[8,768]{1,0:T(8,128)S(1)} %shard_map.81.a_ref), channel_id=1, source_target_pairs={{0,1},{1,2},{2,3},{3,0},{4,5},{5,6},{6,7},{7,4},{8,9},{9,10},{10,1... | collective-permute-start | bytes 73736 | tf_op jit(solution)/shard_map/ppermute | solution.py:243
  56.8 31.6 %collective-permute-start.8 = (f32[768,256]{1,0:T(8,128)S(1)}, f32[768,256]{1,0:T(8,128)S(1)}, u32[]{:S(2)}, u32[]{:S(2)}) collective-permute-start(f32[768,256]{1,0:T(8,128)S(1)} %get-tuple-element.65), channel_id=1, source_target_pairs={{0,16},{16,0},{32,48},{48,32},{64,80},{80,64},{96,112},{112,96},{1... | collective-permute-start | bytes 2359304 | tf_op jit(solution)/shard_map/ppermute | solution.py:239
  64.0 9.9 %copy-start.16 = (f32[64,1024]{1,0:T(8,128)}, f32[64,1024]{1,0:T(8,128)S(1)}, u32[]{:S(2)}) copy-start(f32[64,1024]{1,0:T(8,128)S(1)} %get-tuple-element.73.own_ref) | copy-start | bytes 786436
  64.0 10.6 %collective-permute-start.18 = (f32[32,1024]{1,0:T(8,128)S(1)}, f32[32,1024]{1,0:T(8,128)S(1)}, u32[]{:S(2)}, u32[]{:S(2)}) collective-permute-start(f32[32,1024]{1,0:T(8,128)S(1)} %get-tuple-element.76), channel_id=1, source_target_pairs={{0,32},{16,48},{32,64},{48,80},{64,96},{80,112},{96,0},{112,16},{1... | collective-permute-start | bytes 393224 | tf_op jit(solution)/shard_map/ppermute | solution.py:239
  65.3 9.3 %collective-permute-start.19 = (f32[32,1024]{1,0:T(8,128)S(1)}, f32[32,1024]{1,0:T(8,128)S(1)}, u32[]{:S(2)}, u32[]{:S(2)}) collective-permute-start(f32[32,1024]{1,0:T(8,128)S(1)} %get-tuple-element.77), channel_id=1, source_target_pairs={{0,96},{16,112},{32,0},{48,16},{64,32},{80,48},{96,64},{112,80},{1... | collective-permute-start | bytes 393224 | tf_op jit(solution)/shard_map/ppermute | solution.py:239
  74.6 13.0 %collective-permute-start.25 = (f32[32,1536]{1,0:T(8,128)S(1)}, f32[32,1536]{1,0:T(8,128)S(1)}, u32[]{:S(2)}, u32[]{:S(2)}) collective-permute-start(f32[32,1536]{1,0:T(8,128)S(1)} %get-tuple-element.87), channel_id=1, source_target_pairs={{0,32},{16,48},{32,64},{48,80},{64,96},{80,112},{96,0},{112,16},{1... | collective-permute-start | bytes 589832 | tf_op jit(solution)/shard_map/ppermute | solution.py:239
  76.5 16.3 %collective-permute-start.20 = (f32[64,1024]{1,0:T(8,128)}, f32[64,1024]{1,0:T(8,128)}, u32[]{:S(2)}, u32[]{:S(2)}) collective-permute-start(f32[64,1024]{1,0:T(8,128)} %get-tuple-element.78), channel_id=1, source_target_pairs={{0,32},{16,48},{32,64},{48,80},{64,96},{80,112},{96,0},{112,16},{1... | collective-permute-start | bytes 786440 | tf_op jit(solution)/shard_map/ppermute | solution.py:239
  77.7 13.4 %collective-permute-start.26 = (f32[32,1536]{1,0:T(8,128)}, f32[32,1536]{1,0:T(8,128)}, u32[]{:S(2)}, u32[]{:S(2)}) collective-permute-start(f32[32,1536]{1,0:T(8,128)} %get-tuple-element.88), channel_id=1, source_target_pairs={{0,96},{16,112},{32,0},{48,16},{64,32},{80,48},{96,64},{112,80},{1... | collective-permute-start | bytes 589832 | tf_op jit(solution)/shard_map/ppermute | solution.py:239
  79.2 18.4 %collective-permute-start.21 = (f32[64,1024]{1,0:T(8,128)}, f32[64,1024]{1,0:T(8,128)}, u32[]{:S(2)}, u32[]{:S(2)}) collective-permute-start(f32[64,1024]{1,0:T(8,128)} %get-tuple-element.79), channel_id=1, source_target_pairs={{0,96},{16,112},{32,0},{48,16},{64,32},{80,48},{96,64},{112,80},{1... | collective-permute-start | bytes 786440 | tf_op jit(solution)/shard_map/ppermute | solution.py:239
  88.4 10.3 %collective-permute-start.32 = (f32[32,1536]{1,0:T(8,128)}, f32[32,1536]{1,0:T(8,128)}, u32[]{:S(2)}, u32[]{:S(2)}) collective-permute-start(f32[32,1536]{1,0:T(8,128)} %get-tuple-element.98), channel_id=1, source_target_pairs={{0,32},{16,48},{32,64},{48,80},{64,96},{80,112},{96,0},{112,16},{1... | collective-permute-start | bytes 589832 | tf_op jit(solution)/shard_map/ppermute | solution.py:239
  88.4 13.3 %collective-permute-start.33 = (f32[32,1536]{1,0:T(8,128)}, f32[32,1536]{1,0:T(8,128)}, u32[]{:S(2)}, u32[]{:S(2)}) collective-permute-start(f32[32,1536]{1,0:T(8,128)} %get-tuple-element.99), channel_id=1, source_target_pairs={{0,96},{16,112},{32,0},{48,16},{64,32},{80,48},{96,64},{112,80},{1... | collective-permute-start | bytes 589832 | tf_op jit(solution)/shard_map/ppermute | solution.py:239
  91.1 17.3 %collective-permute-start.9 = (f32[192,256]{1,0:T(8,128)S(1)}, f32[192,256]{1,0:T(8,128)S(1)}, u32[]{:S(2)}, u32[]{:S(2)}) collective-permute-start(f32[192,256]{1,0:T(8,128)S(1)} %get-tuple-element.67), channel_id=1, source_target_pairs={{0,4},{1,5},{2,6},{3,7},{4,8},{5,9},{6,10},{7,11},{8,12},{9,13},{1... | collective-permute-start | bytes 589832 | tf_op jit(solution)/shard_map/ppermute | solution.py:243
  92.7 15.8 %collective-permute-start.10 = (f32[192,256]{1,0:T(8,128)S(1)}, f32[192,256]{1,0:T(8,128)S(1)}, u32[]{:S(2)}, u32[]{:S(2)}) collective-permute-start(f32[192,256]{1,0:T(8,128)S(1)} %get-tuple-element.68), channel_id=1, source_target_pairs={{0,12},{1,13},{2,14},{3,15},{4,0},{5,1},{6,2},{7,3},{8,4},{9,5},{1... | collective-permute-start | bytes 589832 | tf_op jit(solution)/shard_map/ppermute | solution.py:243
  97.6 26.8 %collective-permute-start.27 = (f32[64,1536]{1,0:T(8,128)S(1)}, f32[64,1536]{1,0:T(8,128)S(1)}, u32[]{:S(2)}, u32[]{:S(2)}) collective-permute-start(f32[64,1536]{1,0:T(8,128)S(1)} %get-tuple-element.89), channel_id=1, source_target_pairs={{0,32},{16,48},{32,64},{48,80},{64,96},{80,112},{96,0},{112,16},{1... | collective-permute-start | bytes 1179656 | tf_op jit(solution)/shard_map/ppermute | solution.py:239
  98.7 27.2 %collective-permute-start.28 = (f32[64,1536]{1,0:T(8,128)}, f32[64,1536]{1,0:T(8,128)S(1)}, u32[]{:S(2)}, u32[]{:S(2)}) collective-permute-start(f32[64,1536]{1,0:T(8,128)} %copy-done.15), channel_id=1, source_target_pairs={{0,96},{16,112},{32,0},{48,16},{64,32},{80,48},{96,64},{112,80},{1... | collective-permute-start | bytes 1179656 | tf_op jit(solution)/shard_map/ppermute | solution.py:239
  101.7 5.1 %collective-permute-start.22 = (f32[16,1024]{1,0:T(8,128)S(1)}, f32[16,1024]{1,0:T(8,128)S(1)}, u32[]{:S(2)}, u32[]{:S(2)}) collective-permute-start(f32[16,1024]{1,0:T(8,128)S(1)} %get-tuple-element.81), channel_id=1, source_target_pairs={{0,16},{16,0},{32,48},{48,32},{64,80},{80,64},{96,112},{112,96},{1... | collective-permute-start | bytes 196616 | tf_op jit(solution)/shard_map/ppermute | solution.py:239
  106.8 7.6 %collective-permute-start.11 = (f32[192,256]{1,0:T(8,128)S(1)}, f32[192,256]{1,0:T(8,128)S(1)}, u32[]{:S(2)}, u32[]{:S(2)}) collective-permute-start(f32[192,256]{1,0:T(8,128)S(1)} %get-tuple-element.69), channel_id=1, source_target_pairs={{0,8},{1,9},{2,10},{3,11},{4,12},{5,13},{6,14},{7,15},{8,0},{9,1},... | collective-permute-start | bytes 589832 | tf_op jit(solution)/shard_map/ppermute | solution.py:243
  107.3 47.5 %copy-start.8 = (bf16[768,256]{1,0:T(8,128)(2,1)S(1)}, bf16[768,256]{1,0:T(8,128)(2,1)}, u32[]{:S(2)}) copy-start(bf16[768,256]{1,0:T(8,128)(2,1)} %rows_ref.1) | copy-start | bytes 1179652
  108.5 17.5 %collective-permute-start.34 = (f32[64,1536]{1,0:T(8,128)S(1)}, f32[64,1536]{1,0:T(8,128)S(1)}, u32[]{:S(2)}, u32[]{:S(2)}) collective-permute-start(f32[64,1536]{1,0:T(8,128)S(1)} %get-tuple-element.100), channel_id=1, source_target_pairs={{0,32},{16,48},{32,64},{48,80},{64,96},{80,112},{96,0},{112,16},{1... | collective-permute-start | bytes 1179656 | tf_op jit(solution)/shard_map/ppermute | solution.py:239
  108.6 20.4 %collective-permute-start.35 = (f32[64,1536]{1,0:T(8,128)S(1)}, f32[64,1536]{1,0:T(8,128)S(1)}, u32[]{:S(2)}, u32[]{:S(2)}) collective-permute-start(f32[64,1536]{1,0:T(8,128)S(1)} %get-tuple-element.101), channel_id=1, source_target_pairs={{0,96},{16,112},{32,0},{48,16},{64,32},{80,48},{96,64},{112,80},{1... | collective-permute-start | bytes 1179656 | tf_op jit(solution)/shard_map/ppermute | solution.py:239
  114.4 7.1 %collective-permute-start.23 = (f32[16,1024]{1,0:T(8,128)S(1)}, f32[16,1024]{1,0:T(8,128)S(1)}, u32[]{:S(2)}, u32[]{:S(2)}) collective-permute-start(f32[16,1024]{1,0:T(8,128)S(1)} %get-tuple-element.82), channel_id=1, source_target_pairs={{0,128},{16,144},{32,160},{48,176},{64,192},{80,208},{96,224},{112... | collective-permute-start | bytes 196616 | tf_op jit(solution)/shard_map/ppermute | solution.py:239
  121.6 11.4 %collective-permute-start.14 = (f32[192,256]{1,0:T(8,128)S(1)}, f32[192,256]{1,0:T(8,128)S(1)}, u32[]{:S(2)}, u32[]{:S(2)}) collective-permute-start(f32[192,256]{1,0:T(8,128)S(1)} %shard_map.87.a_ref), channel_id=1, source_target_pairs={{0,3},{1,0},{2,1},{3,2},{4,7},{5,4},{6,5},{7,6},{8,11},{9,8},{10,9... | collective-permute-start | bytes 589832 | tf_op jit(solution)/shard_map/ppermute | solution.py:243
  124.4 23.3 %collective-permute-start.13 = (f32[192,256]{1,0:T(8,128)S(1)}, f32[192,256]{1,0:T(8,128)S(1)}, u32[]{:S(2)}, u32[]{:S(2)}) collective-permute-start(f32[192,256]{1,0:T(8,128)S(1)} %shard_map.87.a_ref), channel_id=1, source_target_pairs={{0,2},{1,3},{2,0},{3,1},{4,6},{5,7},{6,4},{7,5},{8,10},{9,11},{10,... | collective-permute-start | bytes 589832 | tf_op jit(solution)/shard_map/ppermute | solution.py:243
  125.9 28.8 %collective-permute-start.12 = (f32[192,256]{1,0:T(8,128)S(1)}, f32[192,256]{1,0:T(8,128)S(1)}, u32[]{:S(2)}, u32[]{:S(2)}) collective-permute-start(f32[192,256]{1,0:T(8,128)S(1)} %shard_map.87.a_ref), channel_id=1, source_target_pairs={{0,1},{1,2},{2,3},{3,0},{4,5},{5,6},{6,7},{7,4},{8,9},{9,10},{10,1... | collective-permute-start | bytes 589832 | tf_op jit(solution)/shard_map/ppermute | solution.py:243
  126.0 29.5 %collective-permute-start.29 = (f32[16,1536]{1,0:T(8,128)S(1)}, f32[16,1536]{1,0:T(8,128)S(1)}, u32[]{:S(2)}, u32[]{:S(2)}) collective-permute-start(f32[16,1536]{1,0:T(8,128)S(1)} %get-tuple-element.92), channel_id=1, source_target_pairs={{0,16},{16,0},{32,48},{48,32},{64,80},{80,64},{96,112},{112,96},{1... | collective-permute-start | bytes 294920 | tf_op jit(solution)/shard_map/ppermute | solution.py:239
  129.0 28.8 %collective-permute-start.30 = (f32[16,1536]{1,0:T(8,128)S(1)}, f32[16,1536]{1,0:T(8,128)S(1)}, u32[]{:S(2)}, u32[]{:S(2)}) collective-permute-start(f32[16,1536]{1,0:T(8,128)S(1)} %get-tuple-element.93), channel_id=1, source_target_pairs={{0,128},{16,144},{32,160},{48,176},{64,192},{80,208},{96,224},{112... | collective-permute-start | bytes 294920 | tf_op jit(solution)/shard_map/ppermute | solution.py:239
  132.9 22.0 %collective-permute-start.24 = (f32[16,1024]{1,0:T(8,128)S(1)}, f32[16,1024]{1,0:T(8,128)S(1)}, u32[]{:S(2)}, u32[]{:S(2)}) collective-permute-start(f32[16,1024]{1,0:T(8,128)S(1)} %get-tuple-element.83), channel_id=1, source_target_pairs={{0,144},{16,128},{32,176},{48,160},{64,208},{80,192},{96,240},{112... | collective-permute-start | bytes 196616 | tf_op jit(solution)/shard_map/ppermute | solution.py:239
  147.7 10.1 %collective-permute-start.31 = (f32[16,1536]{1,0:T(8,128)S(1)}, f32[16,1536]{1,0:T(8,128)S(1)}, u32[]{:S(2)}, u32[]{:S(2)}) collective-permute-start(f32[16,1536]{1,0:T(8,128)S(1)} %get-tuple-element.94), channel_id=1, source_target_pairs={{0,144},{16,128},{32,176},{48,160},{64,208},{80,192},{96,240},{112... | collective-permute-start | bytes 294920 | tf_op jit(solution)/shard_map/ppermute | solution.py:239
  154.7 4.7 %collective-permute-start.36 = (f32[16,1536]{1,0:T(8,128)S(1)}, f32[16,1536]{1,0:T(8,128)S(1)}, u32[]{:S(2)}, u32[]{:S(2)}) collective-permute-start(f32[16,1536]{1,0:T(8,128)S(1)} %get-tuple-element.103), channel_id=1, source_target_pairs={{0,16},{16,0},{32,48},{48,32},{64,80},{80,64},{96,112},{112,96},{1... | collective-permute-start | bytes 294920 | tf_op jit(solution)/shard_map/ppermute | solution.py:239
  155.0 19.9 %collective-permute-start.17 = (f32[192,256]{1,0:T(8,128)S(1)}, f32[192,256]{1,0:T(8,128)S(1)}, u32[]{:S(2)}, u32[]{:S(2)}) collective-permute-start(f32[192,256]{1,0:T(8,128)S(1)} %shard_map.88.a_ref), channel_id=1, source_target_pairs={{0,8},{1,9},{2,10},{3,11},{4,12},{5,13},{6,14},{7,15},{8,0},{9,1},... | collective-permute-start | bytes 589832 | tf_op jit(solution)/shard_map/ppermute | solution.py:243
  155.5 19.3 %collective-permute-start.16 = (f32[192,256]{1,0:T(8,128)S(1)}, f32[192,256]{1,0:T(8,128)S(1)}, u32[]{:S(2)}, u32[]{:S(2)}) collective-permute-start(f32[192,256]{1,0:T(8,128)S(1)} %shard_map.88.a_ref), channel_id=1, source_target_pairs={{0,12},{1,13},{2,14},{3,15},{4,0},{5,1},{6,2},{7,3},{8,4},{9,5},{1... | collective-permute-start | bytes 589832 | tf_op jit(solution)/shard_map/ppermute | solution.py:243
  157.8 17.1 %collective-permute-start.15 = (f32[192,256]{1,0:T(8,128)S(1)}, f32[192,256]{1,0:T(8,128)S(1)}, u32[]{:S(2)}, u32[]{:S(2)}) collective-permute-start(f32[192,256]{1,0:T(8,128)S(1)} %shard_map.88.a_ref), channel_id=1, source_target_pairs={{0,4},{1,5},{2,6},{3,7},{4,8},{5,9},{6,10},{7,11},{8,12},{9,13},{1... | collective-permute-start | bytes 589832 | tf_op jit(solution)/shard_map/ppermute | solution.py:243
  157.8 8.6 %collective-permute-start.37 = (f32[16,1536]{1,0:T(8,128)S(1)}, f32[16,1536]{1,0:T(8,128)S(1)}, u32[]{:S(2)}, u32[]{:S(2)}) collective-permute-start(f32[16,1536]{1,0:T(8,128)S(1)} %get-tuple-element.104), channel_id=1, source_target_pairs={{0,128},{16,144},{32,160},{48,176},{64,192},{80,208},{96,224},{112... | collective-permute-start | bytes 294920 | tf_op jit(solution)/shard_map/ppermute | solution.py:239
  159.5 14.5 %collective-permute-start.38 = (f32[16,1536]{1,0:T(8,128)S(1)}, f32[16,1536]{1,0:T(8,128)S(1)}, u32[]{:S(2)}, u32[]{:S(2)}) collective-permute-start(f32[16,1536]{1,0:T(8,128)S(1)} %get-tuple-element.105), channel_id=1, source_target_pairs={{0,144},{16,128},{32,176},{48,160},{64,208},{80,192},{96,240},{112... | collective-permute-start | bytes 294920 | tf_op jit(solution)/shard_map/ppermute | solution.py:239
  (17 other events, 32.8 us)

commit v2 on v1

v2 whole, which is shorter than its diff:
```python
import functools
import jax
import jax.numpy as jnp
import numpy as np
from jax import lax
from jax.experimental import pallas as pl
from jax.experimental.pallas import tpu as pltpu
from jax.sharding import PartitionSpec as P

student_temp = 0.1
teacher_temp = 0.04
norm_eps = 1e-06
LOG2E = 1.4426950408889634
F32 = jnp.float32
BF16 = jnp.bfloat16
TILE = 1024
ROWBLK = 768
PART = 512
CHUNKS = (2048, 2048)
MIB = 1 << 20


def call(kernel, out, *args, in_specs, out_specs, after=(), scalars=0, grid=(), scratch_shapes=(), aliases=None,
         vmem=8, flops=0, nbytes=0):
    count, extra = len(args), len(after)

    def body(*refs):
        kernel(*refs[:count], *refs[count + extra :])

    return pl.pallas_call(
        body,
        out_shape=out,
        grid_spec=pltpu.PrefetchScalarGridSpec(
            num_scalar_prefetch=scalars,
            grid=grid,
            in_specs=list(in_specs) + [pl.BlockSpec(memory_space=pl.ANY)] * extra,
            out_specs=out_specs,
            scratch_shapes=scratch_shapes,
        ),
        input_output_aliases=aliases or {},
        compiler_params=pltpu.CompilerParams(vmem_limit_bytes=vmem * MIB),
        cost_estimate=pl.CostEstimate(flops=flops, bytes_accessed=nbytes, transcendentals=0),
    )(*args, *after)


def shape(dims, dtype=F32):
    return jax.ShapeDtypeStruct(dims, dtype)


def prep_kernel(s_ref, t_ref, z_ref):
    size = s_ref.shape[0]
    rows = pl.ds(pl.multiple_of(pl.program_id(0) * size, size), size)
    for i, ref in enumerate((s_ref, t_ref)):
        v = ref[...].astype(F32)
        z_ref[i, rows, :] = v / jnp.sqrt(jnp.sum(v * v, axis=1, keepdims=True) + norm_eps)


def unit_columns(ref):
    v = ref[...].astype(F32)
    inv = 1.0 / jnp.sqrt(jnp.sum(v * v, axis=0, keepdims=True) + norm_eps)
    return (v * inv).astype(BF16), inv


def tile_at(i):
    return pl.ds(pl.multiple_of(i * TILE, TILE), TILE)


def logits_pass(z_ref, ws_ref, wt_ref, center_ref, es_ref, et_ref, sums_ref, zb, acc, last):
    @pl.when(pl.program_id(0) == 0)
    def _():
        zb[...] = z_ref[...].astype(BF16)
        acc[...] = jnp.zeros_like(acc)

    cols = tile_at(pl.program_id(0))
    shift = center_ref[...] * (LOG2E / teacher_temp)
    rows = zb.shape[1]
    for r in range(rows // ROWBLK):
        part = pl.ds(r * ROWBLK, ROWBLK)
        for i, (w_ref, e_ref) in enumerate(((ws_ref, es_ref), (wt_ref, et_ref))):
            logit = jnp.dot(zb[i, part, :], w_ref[:, cols], preferred_element_type=F32)
            if i == 0:
                e = jnp.exp2(logit * (LOG2E / student_temp))
            else:
                e = jnp.exp2(logit * (LOG2E / teacher_temp) - shift)
            total = e[:, :128]
            for k in range(1, TILE // 128):
                total = total + e[:, k * 128 : (k + 1) * 128]
            acc[i, part, :] += total
            e_ref[part, cols] = e.astype(BF16)

    @pl.when(pl.program_id(0) == last)
    def _():
        for i in range(2):
            sums_ref[i : i + 1, :] = jnp.sum(acc[i].T, axis=0, keepdims=True)


def own_kernel(last, core_ref, z_ref, sp_ref, tp_ref, center_ref,
               es_ref, et_ref, ws_ref, wt_ref, inv_ref, sums_ref, zb, acc):
    cols = tile_at(pl.program_id(0))
    w_s, inv = unit_columns(sp_ref)
    w_t, _ = unit_columns(tp_ref)
    ws_ref[:, cols] = w_s
    wt_ref[:, cols] = w_t
    inv_ref[:, cols] = inv
    logits_pass(z_ref, ws_ref, wt_ref, center_ref, es_ref, et_ref, sums_ref, zb, acc, last)


def other_kernel(last, core_ref, z_ref, ws_ref, wt_ref, center_ref, mine_ref, weight_ref,
                 es_ref, et_ref, pay_ref, zb, acc):
    logits_pass(z_ref, ws_ref, wt_ref, center_ref, es_ref, et_ref, pay_ref.at[2:4], zb, acc, last)

    @pl.when(pl.program_id(0) == 0)
    def _():
        pay_ref[0:2, :] = mine_ref[...]
        pay_ref[4:5, :] = weight_ref[...]
        pay_ref[5:8, :] = jnp.zeros_like(pay_ref[5:8, :])


def chip_kernel(mine_ref, theirs_ref, out_ref):
    out_ref[0:2, :] = mine_ref[0:2, :] + theirs_ref[2:4, :]
    out_ref[2:4, :] = mine_ref[2:4, :] + theirs_ref[0:2, :]
    out_ref[4:5, :] = mine_ref[4:5, :]
    out_ref[5:6, :] = theirs_ref[4:5, :]
    out_ref[6:8, :] = jnp.zeros_like(out_ref[6:8, :])


def add4_kernel(a_ref, b_ref, c_ref, d_ref, out_ref):
    out_ref[0:4, :] = a_ref[0:4, :] + b_ref[0:4, :] + c_ref[0:4, :] + d_ref[0:4, :]
    out_ref[4:8, :] = a_ref[4:8, :]


def scale_kernel(a_ref, b_ref, c_ref, d_ref, zo_ref, zx_ref, u_ref, out_ref, f_ref, mix_ref, fac):
    total = a_ref[0:4, :] + b_ref[0:4, :] + c_ref[0:4, :] + d_ref[0:4, :]
    rows = total.shape[1]
    for i in range(4):
        weight = a_ref[4 + i // 2 : 5 + i // 2, :]
        f = weight / (total[i : i + 1, :] * student_temp)
        if i % 2:
            f = -f
        f_ref[i : i + 1, :] = f
        z_ref = zo_ref if i < 2 else zx_ref
        out_ref[:, i * rows : (i + 1) * rows] = (z_ref[...].astype(F32) * f).astype(BF16)
    mix_kernel(f_ref, u_ref, mix_ref, fac)


def unit_kernel(es_ref, et_ref, ws_ref, z_ref, perm_ref, u_ref, zt_ref):
    zt_ref[...] = lax.dot_general(
        perm_ref[...], z_ref[0].astype(BF16), (((1,), (1,)), ((), ())), preferred_element_type=F32
    ).astype(BF16)
    for i, ref in enumerate((es_ref, et_ref)):
        u_ref[i] = lax.dot_general(
            ref[...], ws_ref[...], (((1,), (1,)), ((), ())), preferred_element_type=F32
        )


def fill_columns(f_ref, first, fac):
    for i in range(2):
        fac[i] = jnp.broadcast_to(f_ref[first + i : first + i + 1, :], (128, fac.shape[1])).T


def mix_kernel(f_ref, u_ref, out_ref, fac):
    fill_columns(f_ref, 2, fac)
    for k in range(2):
        lanes = slice(k * 128, (k + 1) * 128)
        out_ref[:, lanes] = fac[0] * u_ref[0, :, lanes] + fac[1] * u_ref[1, :, lanes]


def combine_kernel(x_ref, f_ref, u_ref, got_ref, o0_ref, op_ref, om_ref, o2_ref, fac):
    fill_columns(f_ref, 0, fac)
    size = o0_ref.shape[0]
    for step, ref in ((0, o0_ref), (1, op_ref), (3, om_ref), (2, o2_ref)):
        rows = pl.ds(pl.multiple_of(lax.rem(x_ref[0] + step, 4) * size, 16), size)
        for k in range(2):
            lanes = slice(k * 128, (k + 1) * 128)
            ref[:, lanes] = (
                fac[0, rows, :] * u_ref[0, rows, lanes] + fac[1, rows, :] * u_ref[1, rows, lanes]
            ) + got_ref[rows, lanes]


def grad_kernel(blocks_ref, z_ref, eso_ref, eto_ref, esx_ref, etx_ref, ws_ref, inv_ref,
                own_ref, bp_ref, bm_ref, ap_ref, am_ref):
    rows = eso_ref.shape[0]
    grad = None
    for i, ref in enumerate((eso_ref, eto_ref, esx_ref, etx_ref)):
        term = jnp.dot(z_ref[:, i * rows : (i + 1) * rows], ref[...], preferred_element_type=F32)
        grad = term if grad is None else grad + term
    w = [ws_ref[pl.ds(pl.multiple_of(blocks_ref[i] * 16, 16), 16), :].astype(F32) for i in range(16)]
    dot = w[0] * grad[0:16]
    for i in range(1, 16):
        dot = dot + w[i] * grad[i * 16 : (i + 1) * 16]
    dot = jnp.sum(dot, axis=0, keepdims=True)
    inv = inv_ref[...]
    homes = (
        [(own_ref, i * 16) for i in range(4)]
        + [(bp_ref, i * 16) for i in range(4)]
        + [(bm_ref, i * 16) for i in range(4)]
        + [(ap_ref, 0), (ap_ref, 16), (am_ref, 0), (am_ref, 16)]
    )
    for i, (ref, at) in enumerate(homes):
        ref[at : at + 16, :] = (grad[i * 16 : (i + 1) * 16] - w[i] * dot) * inv


def ring_kernel(bp_ref, bm_ref, ap_ref, am_ref, rp_ref, rm_ref, op_ref, om_ref):
    op_ref[0:32, :] = bp_ref[0:32, :] + rp_ref[...]
    op_ref[32:64, :] = bp_ref[32:64, :]
    op_ref[64:96, :] = ap_ref[...]
    om_ref[0:32, :] = bm_ref[0:32, :]
    om_ref[32:64, :] = bm_ref[32:64, :] + rm_ref[...]
    om_ref[64:96, :] = am_ref[...]


def ring_last_kernel(bp_ref, bm_ref, rp_ref, rm_ref, op_ref, om_ref):
    op_ref[0:32, :] = bp_ref[0:32, :] + rp_ref[64:96, :]
    op_ref[32:64, :] = bp_ref[32:64, :]
    om_ref[0:32, :] = bm_ref[0:32, :]
    om_ref[32:64, :] = bm_ref[32:64, :] + rm_ref[64:96, :]


def ring_end_kernel(own_ref, rp_ref, rm_ref, k_ref, c_ref, z_ref):
    for at, ref in ((0, k_ref), (16, c_ref), (32, z_ref)):
        rows = slice(at, at + ref.shape[0])
        ref[...] = own_ref[rows, :] + rp_ref[rows, :] + rm_ref[rows, :]


def ring_end_last_kernel(own_ref, rp_ref, rm_ref, before_ref, got_ref, k_ref, c_ref, z_ref, zc_ref):
    width = k_ref.shape[1]
    c_ref[:, 0 : before_ref.shape[1]] = before_ref[...] + got_ref[16:32, :]
    for i, ref in enumerate((k_ref, c_ref.at[:, c_ref.shape[1] - width :], z_ref, zc_ref)):
        rows = slice(i * 16, (i + 1) * 16)
        ref[...] = own_ref[rows, :] + rp_ref[rows, :] + rm_ref[rows, :]


def protos_kernel(core_ref, k0_ref, z0_ref, k1_ref, z1_ref, x1_ref, c_ref, out_ref):
    half = out_ref.shape[1] // 2
    at = k0_ref.shape[1]
    mine = core_ref[0] * half
    theirs = (1 - core_ref[0]) * half
    columns = lambda start, width: pl.ds(pl.multiple_of(start, 128), width)
    out_ref[:, columns(mine, at)] = k0_ref[...] + z0_ref[0:16, :]
    out_ref[:, columns(theirs, at)] = c_ref[:, 0:at]
    out_ref[:, columns(mine + at, half - at)] = k1_ref[...] + z1_ref[...]
    out_ref[:, columns(theirs + at, half - at)] = c_ref[:, at:half] + x1_ref[...]


def sum4_kernel(a_ref, b_ref, c_ref, d_ref, out_ref):
    out_ref[...] = a_ref[...] + b_ref[...] + c_ref[...] + d_ref[...]


def rows_kernel(x_ref, a_ref, b_ref, c_ref, d_ref, rows_ref, out_ref):
    total = a_ref[...] + b_ref[...] + c_ref[...] + d_ref[...]
    v = rows_ref[...].astype(F32)
    norm = jnp.sqrt(jnp.sum(v * v, axis=1, keepdims=True) + norm_eps)
    z = v / norm
    out_ref[...] = (total - z * jnp.sum(z * total, axis=1, keepdims=True)) / norm


def place_kernel(x_ref, a_ref, p_ref, m_ref, t_ref, out_ref):
    size = a_ref.shape[0]
    for step, ref in ((0, a_ref), (3, p_ref), (1, m_ref), (2, t_ref)):
        rows = pl.ds(pl.multiple_of(lax.rem(x_ref[0] + step, 4) * size, 16), size)
        out_ref[rows, :] = ref[...]


def dp_pairs(move):
    def at(z, y, c):
        return (z * 4 + y) * 2 + c
    return [(at(z, y, c), at(*move(z, y, c))) for z in range(2) for y in range(4) for c in range(2)]


def mp_pairs(dx, dz):
    return [(x * 4 + z, (x + dx) % 4 * 4 + (z + dz) % 4) for x in range(4) for z in range(4)]


CORE = dp_pairs(lambda z, y, c: (z, y, 1 - c))
YP = dp_pairs(lambda z, y, c: (z, (y + 1) % 4, c))
YM = dp_pairs(lambda z, y, c: (z, (y - 1) % 4, c))
ZZ = dp_pairs(lambda z, y, c: (1 - z, y, c))
ZZC = dp_pairs(lambda z, y, c: (1 - z, y, 1 - c))


def to_dp(v, pairs):
    return lax.ppermute(v, "dp", pairs)


def to_mp(v, dx, dz):
    return lax.ppermute(v, "mp", mp_pairs(dx, dz))


VM = pl.BlockSpec(memory_space=pltpu.VMEM)
SM = pl.BlockSpec(memory_space=pltpu.SMEM)


def local(student_rows, teacher_rows, student_protos, teacher_protos, center, row_weight):
    rows, feats = student_rows.shape
    protos = student_protos.shape[1]
    half = protos // 2
    dp = lax.axis_index("dp")
    core, y, z_hi = dp % 2, dp // 2 % 4, dp // 8
    x = lax.axis_index("mp") // 4
    core_s = core.astype(jnp.int32)[None]
    x_s = x.astype(jnp.int32)[None]
    blocks = jnp.stack([
        ((z_hi ^ zr) * 4 + (y + yr) % 4) * 2 + (core ^ cr)
        for yr in (0, 1, 3, 2) for zr in (0, 1) for cr in (0, 1)
    ]).astype(jnp.int32)
    source = jnp.repeat(blocks, 16) * 16 + jnp.arange(feats, dtype=jnp.int32) % 16
    perm = (source[:, None] == jnp.arange(feats, dtype=jnp.int32)[None, :]).astype(BF16)
    hbm = lambda v: pltpu.with_memory_space_constraint(v, pltpu.HBM)

    row_tile = pl.BlockSpec((rows // 2, feats), lambda i: (i, 0))
    z = call(prep_kernel, shape((2, rows, feats)), hbm(student_rows), hbm(teacher_rows), grid=(2,),
             in_specs=[row_tile, row_tile], out_specs=VM, nbytes=3 * MIB)
    z_other = to_dp(z, CORE)

    tiles = half // TILE
    center2 = center[None, :]
    weight2 = row_weight[None, :]
    wide = lambda i, c: (0, c[0] * tiles + i)
    w_wide = pl.BlockSpec((feats, TILE), wide)
    e_shape = pltpu.VMEM((rows, half), BF16)
    w_shape = shape((feats, half), BF16)
    pass_scratch = (pltpu.VMEM((2, rows, feats), BF16), pltpu.VMEM((2, rows, 128), F32))
    flops = 4 * rows * feats * half
    es_o, et_o, ws, wt, inv, sums = call(
        functools.partial(own_kernel, tiles - 1),
        (e_shape, e_shape, w_shape, w_shape, shape((1, half)), shape((2, rows))),
        core_s, z, hbm(student_protos), hbm(teacher_protos), center2,
        scalars=1, grid=(tiles,), in_specs=[VM, w_wide, w_wide, pl.BlockSpec((1, TILE), wide)],
        out_specs=[VM] * 6, scratch_shapes=pass_scratch,
        vmem=14, flops=flops, nbytes=8 * MIB,
    )
    es_x, et_x, pay = call(
        functools.partial(other_kernel, tiles - 1),
        (e_shape, e_shape, shape((8, rows))),
        core_s, z_other, ws, wt, center2, sums, weight2,
        scalars=1, grid=(tiles,), in_specs=[VM, VM, VM, pl.BlockSpec((1, TILE), wide), VM, VM],
        out_specs=[VM] * 3, scratch_shapes=pass_scratch,
        vmem=14, flops=flops, nbytes=8 * MIB,
    )
    small = dict(in_specs=[VM] * 2, out_specs=VM)
    small4 = dict(in_specs=[VM] * 4, out_specs=VM)

    tot1 = call(chip_kernel, shape((8, rows)), pay, to_dp(pay, CORE), **small)
    tot2 = call(add4_kernel, shape((8, rows)), tot1, *[to_mp(tot1, k, 0) for k in (1, 2, 3)], **small4)
    tot = [tot2] + [to_mp(tot2, 0, k) for k in (1, 2, 3)]

    def unit(es, et, zz, after):
        return call(
            unit_kernel, (shape((2, rows, feats)), shape((feats, rows), BF16)), es, et, ws, zz, perm,
            in_specs=[VM] * 5, out_specs=[VM] * 2, after=after, vmem=16, flops=flops, nbytes=8 * MIB,
        )

    u_x, zt_x = unit(es_x, et_x, z_other, (tot1,))
    u_o, zt_o = unit(es_o, et_o, z, (tot2,))
    fac = [pltpu.VMEM((2, rows, 128), F32)]
    zs, f, mixed = call(scale_kernel, (shape((feats, 4 * rows), BF16), shape((4, rows)), shape((rows, feats))), *tot, zt_o, zt_x, u_x,
                        in_specs=[VM] * 7, out_specs=[VM] * 3, scratch_shapes=fac)
    got = to_dp(mixed, CORE)

    def chunk(at, width, after):
        first = at // PART
        own = lambda i, b: (0, i)
        col = lambda i, b: (0, first + i)
        e_tile = pl.BlockSpec((rows, PART), col)
        return call(
            grad_kernel, (*[shape((64, width))] * 3, *[shape((32, width))] * 2),
            blocks, zs, hbm(es_o), hbm(et_o), hbm(es_x), hbm(et_x), ws, inv,
            scalars=1, grid=(width // PART,),
            in_specs=[VM] + [e_tile] * 4 + [pl.BlockSpec((feats, PART), col), pl.BlockSpec((1, PART), col)],
            out_specs=[pl.BlockSpec((64, PART), own)] * 3 + [pl.BlockSpec((32, PART), own)] * 2,
            after=after, vmem=24, flops=2 * flops * width // half, nbytes=26 * MIB * width // half,
        )

    quarter = shape((rows // 4, feats))
    w0, w1 = CHUNKS
    own0, bp0, bm0, ap0, am0 = chunk(0, w0, ())
    o0, op, om, o2 = call(combine_kernel, (quarter,) * 4, x_s, f, u_o, got, after=(ap0,),
                          in_specs=[SM, VM, VM, VM], out_specs=[VM] * 4, scratch_shapes=fac)
    own1, bp1, bm1, ap1, am1 = chunk(w0, w1, (o0,))
    part = call(sum4_kernel, quarter, o0, to_mp(op, 1, 0), to_mp(om, 3, 0), to_mp(o2, 2, 0), **small4)
    mp, mm = call(ring_kernel, (shape((96, w0)),) * 2, bp0, bm0, ap1, am1, to_dp(ap0, YP), to_dp(am0, YM),
                  after=(part,), in_specs=[VM] * 6, out_specs=[VM] * 2)
    gp, gm = to_dp(mp, YP), to_dp(mm, YM)
    fixed = pl.BlockSpec((rows // 4, feats), lambda i, c: (0, 0))
    mine = call(rows_kernel, quarter, x_s, part, *[to_mp(part, 0, k) for k in (1, 2, 3)], hbm(student_rows),
                scalars=1, grid=(1,), in_specs=[fixed] * 4 + [pl.BlockSpec((rows // 4, feats), lambda i, c: (c[0], 0))],
                out_specs=fixed)
    bp1, bm1 = call(ring_last_kernel, (shape((64, w1)),) * 2, bp1, bm1, gp, gm, after=(mine,),
                    in_specs=[VM] * 4, out_specs=[VM] * 2)
    keep0, c0, zz0 = call(ring_end_kernel, (shape((16, w0)), shape((16, w0)), shape((32, w0))), own0, gp, gm,
                          after=(bp1,), in_specs=[VM] * 3, out_specs=[VM] * 3)
    got0 = to_dp(zz0, ZZ)
    keep1, c1, zz1, zc1 = call(
        ring_end_last_kernel, (shape((16, w1)), shape((16, half)), shape((16, w1)), shape((16, w1))),
        own1, to_dp(bp1, YP), to_dp(bm1, YM), c0, got0, in_specs=[VM] * 5, out_specs=[VM] * 4)
    parts = [keep0, got0, keep1, to_dp(zz1, ZZ), to_dp(zc1, ZZC), to_dp(c1, CORE)]
    grad_rows = call(place_kernel, shape((rows, feats)), x_s, mine, to_mp(mine, 1, 0), to_mp(mine, 3, 0), to_mp(mine, 2, 0),
                     in_specs=[SM] + [VM] * 4, out_specs=VM)
    proto_grad = call(protos_kernel, shape((16, protos)), core_s, *parts,
                      in_specs=[SM] + [VM] * len(parts), out_specs=VM)
    return grad_rows, proto_grad


def solution(mesh):
    placed = (P("dp", None), P("dp", None), P(None, "mp"), P(None, "mp"), P("mp"), P("dp"))
    return jax.shard_map(
        local, mesh=mesh, in_specs=placed, out_specs=(P("dp", None), P("dp", "mp")), check_vma=False
    )
```

time: 177 us -> 130 us (0.73)
  the two profiles are of different devices: /device:TPU:1 before, /device:TPU:32 now
where the time goes in v2:
time: 130 us; the launch traced here: 128 us
  Pallas kernels  49 us (38%)
  starting transfers between devices  41.7 us (32%)
  waiting for transfers between devices  33 us (25%)
  local copies, waits for them, and re-layouts  2.84 us (2%)
    pallas_call x19, Pallas kernels, call(): pl.pallas_call(body, out_shape=out, grid_spec=pltpu.PrefetchScalarGridSpe...  49 us
    ppermute x15, starting transfers between devices, to_mp(): return lax.ppermute(v, 'mp', mp_pairs(dx, dz))  22.5 us
    ppermute x13, starting transfers between devices, to_dp(): return lax.ppermute(v, 'dp', pairs)  19.2 us
    ppermute x15, waiting for transfers between devices, to_mp(): return lax.ppermute(v, 'mp', mp_pairs(dx, dz))  17.1 us
    ppermute x13, waiting for transfers between devices, to_dp(): return lax.ppermute(v, 'dp', pairs)  15.8 us
  transfers between devices with their start and end apart: 28, of which 8 were waited for; matrix products, arithmetic and copies ran while one was open for 0% of the time, Pallas kernels for 29%

profile of v2, /device:TPU:32, one launch (start us, length us, event | category | flops | bytes accessed | tf_op | source)
XLA Modules:
  0.0 127.7 jit_solution(6631616138446305758)
XLA Ops:
  0.7 2.7 %shard_map.77.refs_1_.refs_3_ = f32[2,768,256]{2,1,0:T(8,128)} custom-call(bf16[768,256]{1,0:T(8,128)(2,1)} %refs_5_.1, bf16[768,256]{1,0:T(8,128)(2,1)} %refs_1_.1), custom_call_target="tpu_custom_call" | custom-call | bytes 3145728 | tf_op jit(solution)/shard_map/pallas_call | solution.py:30
  3.3 0.1 stack.67.refs_0_
  3.6 8.0 %shard_map.78 = (bf16[768,4096]{1,0:T(8,128)(2,1)S(1)}, bf16[768,4096]{1,0:T(8,128)(2,1)S(1)}, bf16[256,4096]{1,0:T(8,128)(2,1)S(1)}, bf16[256,4096]{1,0:T(8,128...) custom-call(s32[1]{0:T(128)} %bitcast.1.refs_0_, f32[2,768,256]{2,1,0:T(8,128)} %shard_map.77.refs_1_.refs_3_, ...), custom_call_target="tpu_custom_call" | custom-call | flops 3221225472 | bytes 8388608 | tf_op jit(solution)/shard_map/pallas_call | solution.py:30
  11.7 7.3 %shard_map.79 = (bf16[768,4096]{1,0:T(8,128)(2,1)S(1)}, bf16[768,4096]{1,0:T(8,128)(2,1)S(1)}, f32[8,768]{1,0:T(8,128)S(1)}) custom-call(s32[1]{0:T(128)} %bitcast.1.refs_0_, f32[2,768,256]{2,1,0:T(8,128)} %collective-permute-done.refs_1_.refs_3_, bf16[256,4096]{1,0:T(8,128)(2,1)S(1)} %get-tuple-element.43.refs_2_.refs_6_, ...), custom_call_target="tpu_custom_call" | custom-call | flops 3221225472 | bytes 8388608 | tf_op jit(solution)/shard_map/pallas_call | solution.py:30
  19.0 0.6 collective-permute-start.1
  19.6 0.1 fusion.refs_4_
  19.7 0.7 collective-permute-done.1.refs_1_
  20.5 2.8 %collective-permute-start.4 = (f32[8,768]{1,0:T(8,128)S(1)}, f32[8,768]{1,0:T(8,128)S(1)}, u32[]{:S(2)}, u32[]{:S(2)}) collective-permute-start(f32[8,768]{1,0:T(8,128)S(1)} %shard_map.80.refs_0_.refs_5_), channel_id=1, source_target_pairs={{0,12},{1,13},{2,14},{3,15},{4,0},{5,1},{6,2},{7,3},{8,4},{9,5},{1... | collective-permute-start | bytes 73736 | tf_op jit(solution)/shard_map/ppermute | solution.py:286
  23.3 0.8 collective-permute-start.3
  24.1 0.9 collective-permute-start.2
  25.0 4.9 %shard_map.83 = (f32[2,768,256]{2,1,0:T(8,128)S(1)}, bf16[256,768]{1,0:T(8,128)(2,1)S(1)}) custom-call(bf16[768,4096]{1,0:T(8,128)(2,1)S(1)} %get-tuple-element.50.refs_0_.refs_4_, bf16[768,4096]{1,0:T(8,128)(2,1)S(1)} %get-tuple-element.51.refs_1_.refs_5_, bf16[256,4096]{1,0:T(8,128)(2,1)S(1)} %get-tuple-element.43.refs_2_.refs_6_, ...), custom_call_target="tpu_custom_call" | custom-call | flops 3221225472 | bytes 8388608 | tf_op jit(solution)/shard_map/pallas_call | solution.py:30
  30.0 0.2 collective-permute-start.7
  30.2 3.3 %collective-permute-start.6 = (f32[8,768]{1,0:T(8,128)S(1)}, f32[8,768]{1,0:T(8,128)S(1)}, u32[]{:S(2)}, u32[]{:S(2)}) collective-permute-start(f32[8,768]{1,0:T(8,128)S(1)} %shard_map.81.refs_5_.refs_0_), channel_id=1, source_target_pairs={{0,2},{1,3},{2,0},{3,1},{4,6},{5,7},{6,4},{7,5},{8,10},{9,11},{10,... | collective-permute-start | bytes 73736 | tf_op jit(solution)/shard_map/ppermute | solution.py:286
  33.5 2.8 %collective-permute-start.5 = (f32[8,768]{1,0:T(8,128)S(1)}, f32[8,768]{1,0:T(8,128)S(1)}, u32[]{:S(2)}, u32[]{:S(2)}) collective-permute-start(f32[8,768]{1,0:T(8,128)S(1)} %shard_map.81.refs_5_.refs_0_), channel_id=1, source_target_pairs={{0,1},{1,2},{2,3},{3,0},{4,5},{5,6},{6,7},{7,4},{8,9},{9,10},{10,1... | collective-permute-start | bytes 73736 | tf_op jit(solution)/shard_map/ppermute | solution.py:286
  36.3 4.9 %shard_map.82 = (f32[2,768,256]{2,1,0:T(8,128)S(1)}, bf16[256,768]{1,0:T(8,128)(2,1)S(1)}) custom-call(bf16[768,4096]{1,0:T(8,128)(2,1)S(1)} %get-tuple-element.47.refs_0_.refs_2_, bf16[768,4096]{1,0:T(8,128)(2,1)S(1)} %get-tuple-element.48.refs_1_.refs_3_, bf16[256,4096]{1,0:T(8,128)(2,1)S(1)} %get-tuple-element.43.refs_2_.refs_6_, ...), custom_call_target="tpu_custom_call" | custom-call | flops 3221225472 | bytes 8388608 | tf_op jit(solution)/shard_map/pallas_call | solution.py:30
  41.3 1.5 %shard_map.84 = (bf16[256,3072]{1,0:T(8,128)(2,1)S(1)}, f32[4,768]{1,0:T(4,128)S(1)}, f32[768,256]{1,0:T(8,128)}) custom-call(f32[8,768]{1,0:T(8,128)S(1)} %shard_map.81.refs_5_.refs_0_, f32[8,768]{1,0:T(8,128)S(1)} %collective-permute-done.5.refs_1_, f32[8,768]{1,0:T(8,128)S(1)} %collective-permute-done.6.refs_2_, ...), custom_call_target="tpu_custom_call" | custom-call | tf_op jit(solution)/shard_map/pallas_call | solution.py:30
  42.8 1.1 copy-done.4
  43.9 1.4 %copy-done.5 = bf16[256,3072]{1,0:T(8,128)(2,1)S(1)} copy-done((bf16[256,3072]{1,0:T(8,128)(2,1)S(1)}, bf16[256,3072]{1,0:T(8,128)(2,1)}, u32[]{:S(2)}) %copy-start.5) | copy-done | bytes 1572888
  45.3 7.9 %shard_map.85 = (f32[64,2048]{1,0:T(8,128)S(1)}, f32[64,2048]{1,0:T(8,128)S(1)}, f32[64,2048]{1,0:T(8,128)S(1)}, f32[32,2048]{1,0:T(8,128)S(1)}, f32[32,2048]{1,0:T(8,128)S(1)}) custom-call(s32[16]{0:T(128)S(1)} %stack.67.refs_0_, bf16[256,3072]{1,0:T(8,128)(2,1)S(1)} %copy-done.5, bf16[768,4096]{1,0:T(8,128)(2,1)} %copy-done, bf16[768,4096]{1,0:T(8,128)(2,1)} %copy-done.1, ...), custom_call_target="tpu_custom_call" | custom-call | flops 3221225472 | bytes 13631488 | tf_op jit(solution)/shard_map/pallas_call | solution.py:30
  53.2 3.1 %collective-permute-start.19 = (f32[32,2048]{1,0:T(8,128)S(1)}, f32[32,2048]{1,0:T(8,128)S(1)}, u32[]{:S(2)}, u32[]{:S(2)}) collective-permute-start(f32[32,2048]{1,0:T(8,128)S(1)} %get-tuple-element.69), channel_id=1, source_target_pairs={{0,96},{16,112},{32,0},{48,16},{64,32},{80,48},{96,64},{112,80},{1... | collective-permute-start | bytes 786440 | tf_op jit(solution)/shard_map/ppermute | solution.py:282
  56.3 0.5 shard_map.86
  56.8 1.9 %collective-permute-start.9 = (f32[192,256]{1,0:T(8,128)S(1)}, f32[192,256]{1,0:T(8,128)S(1)}, u32[]{:S(2)}, u32[]{:S(2)}) collective-permute-start(f32[192,256]{1,0:T(8,128)S(1)} %get-tuple-element.61), channel_id=1, source_target_pairs={{0,4},{1,5},{2,6},{3,7},{4,8},{5,9},{6,10},{7,11},{8,12},{9,13},{1... | collective-permute-start | bytes 589832 | tf_op jit(solution)/shard_map/ppermute | solution.py:286
  58.7 1.4 %collective-permute-start.10 = (f32[192,256]{1,0:T(8,128)S(1)}, f32[192,256]{1,0:T(8,128)S(1)}, u32[]{:S(2)}, u32[]{:S(2)}) collective-permute-start(f32[192,256]{1,0:T(8,128)S(1)} %get-tuple-element.62), channel_id=1, source_target_pairs={{0,12},{1,13},{2,14},{3,15},{4,0},{5,1},{6,2},{7,3},{8,4},{9,5},{1... | collective-permute-start | bytes 589832 | tf_op jit(solution)/shard_map/ppermute | solution.py:286
  60.1 0.7 collective-permute-start.11
  60.9 7.9 %shard_map.90 = (f32[64,2048]{1,0:T(8,128)S(1)}, f32[64,2048]{1,0:T(8,128)S(1)}, f32[64,2048]{1,0:T(8,128)S(1)}, f32[32,2048]{1,0:T(8,128)S(1)}, f32[32,2048]{1,0:T(8,128)S(1)}) custom-call(s32[16]{0:T(128)S(1)} %stack.67.refs_0_, bf16[256,3072]{1,0:T(8,128)(2,1)S(1)} %copy-done.5, bf16[768,4096]{1,0:T(8,128)(2,1)} %copy-done, bf16[768,4096]{1,0:T(8,128)(2,1)} %copy-done.1, ...), custom_call_target="tpu_custom_call" | custom-call | flops 3221225472 | bytes 13631488 | tf_op jit(solution)/shard_map/pallas_call | solution.py:30
  68.8 1.1 collective-permute-done.11.refs_3_
  70.0 0.1 shard_map.91
  70.1 0.4 collective-permute-start.20
  70.5 2.9 %collective-permute-start.21 = (f32[96,2048]{1,0:T(8,128)S(1)}, f32[96,2048]{1,0:T(8,128)S(1)}, u32[]{:S(2)}, u32[]{:S(2)}) collective-permute-start(f32[96,2048]{1,0:T(8,128)S(1)} %get-tuple-element.71), channel_id=1, source_target_pairs={{0,96},{16,112},{32,0},{48,16},{64,32},{80,48},{96,64},{112,80},{1... | collective-permute-start | bytes 2359304 | tf_op jit(solution)/shard_map/ppermute | solution.py:282
  73.4 1.5 %collective-permute-start.13 = (f32[192,256]{1,0:T(8,128)S(1)}, f32[192,256]{1,0:T(8,128)S(1)}, u32[]{:S(2)}, u32[]{:S(2)}) collective-permute-start(f32[192,256]{1,0:T(8,128)S(1)} %shard_map.87.refs_1_.refs_6_), channel_id=1, source_target_pairs={{0,2},{1,3},{2,0},{3,1},{4,6},{5,7},{6,4},{7,5},{8,10},{9,11},{10,... | collective-permute-start | bytes 589832 | tf_op jit(solution)/shard_map/ppermute | solution.py:286
  74.9 2.3 %collective-permute-start.12 = (f32[192,256]{1,0:T(8,128)S(1)}, f32[192,256]{1,0:T(8,128)S(1)}, u32[]{:S(2)}, u32[]{:S(2)}) collective-permute-start(f32[192,256]{1,0:T(8,128)S(1)} %shard_map.87.refs_1_.refs_6_), channel_id=1, source_target_pairs={{0,1},{1,2},{2,3},{3,0},{4,5},{5,6},{6,7},{7,4},{8,9},{9,10},{10,1... | collective-permute-start | bytes 589832 | tf_op jit(solution)/shard_map/ppermute | solution.py:286
  77.3 12.1 %collective-permute-done.14.refs_4_ = f32[192,256]{1,0:T(8,128)S(1)} collective-permute-done((f32[192,256]{1,0:T(8,128)S(1)}, f32[192,256]{1,0:T(8,128)S(1)}, u32[]{:S(2)}, u32[]{:S(2)}) %collective-permute-start.14) | collective-permute-done | bytes 196640 | tf_op jit(solution)/shard_map/ppermute | solution.py:286
  89.4 1.1 collective-permute-done.12.refs_2_
  90.5 1.1 shard_map.88.refs_1_.refs_4_
  91.7 1.7 %collective-permute-start.24 = (f32[64,2048]{1,0:T(8,128)S(1)}, f32[64,2048]{1,0:T(8,128)S(1)}, u32[]{:S(2)}, u32[]{:S(2)}) collective-permute-start(f32[64,2048]{1,0:T(8,128)S(1)} %get-tuple-element.78), channel_id=1, source_target_pairs={{0,96},{16,112},{32,0},{48,16},{64,32},{80,48},{96,64},{112,80},{1... | collective-permute-start | bytes 1572872 | tf_op jit(solution)/shard_map/ppermute | solution.py:282
  93.4 0.4 collective-permute-start.23
  93.9 4.8 %collective-permute-start.22 = (f32[32,2048]{1,0:T(8,128)S(1)}, f32[32,2048]{1,0:T(8,128)S(1)}, u32[]{:S(2)}, u32[]{:S(2)}) collective-permute-start(f32[32,2048]{1,0:T(8,128)S(1)} %get-tuple-element.76), channel_id=1, source_target_pairs={{0,128},{16,144},{32,160},{48,176},{64,192},{80,208},{96,224},{112... | collective-permute-start | bytes 786440 | tf_op jit(solution)/shard_map/ppermute | solution.py:282
  98.8 1.7 %collective-permute-start.17 = (f32[192,256]{1,0:T(8,128)S(1)}, f32[192,256]{1,0:T(8,128)S(1)}, u32[]{:S(2)}, u32[]{:S(2)}) collective-permute-start(f32[192,256]{1,0:T(8,128)S(1)} %shard_map.88.refs_1_.refs_4_), channel_id=1, source_target_pairs={{0,8},{1,9},{2,10},{3,11},{4,12},{5,13},{6,14},{7,15},{8,0},{9,1},... | collective-permute-start | bytes 589832 | tf_op jit(solution)/shard_map/ppermute | solution.py:286
  100.5 9.1 %collective-permute-done.22.refs_4_.refs_2_ = f32[32,2048]{1,0:T(8,128)S(1)} collective-permute-done((f32[32,2048]{1,0:T(8,128)S(1)}, f32[32,2048]{1,0:T(8,128)S(1)}, u32[]{:S(2)}, u32[]{:S(2)}) %collective-permute-start.22) | collective-permute-done | bytes 262176 | tf_op jit(solution)/shard_map/ppermute | solution.py:282
  109.8 1.9 %collective-permute-start.16 = (f32[192,256]{1,0:T(8,128)S(1)}, f32[192,256]{1,0:T(8,128)S(1)}, u32[]{:S(2)}, u32[]{:S(2)}) collective-permute-start(f32[192,256]{1,0:T(8,128)S(1)} %shard_map.88.refs_1_.refs_4_), channel_id=1, source_target_pairs={{0,12},{1,13},{2,14},{3,15},{4,0},{5,1},{6,2},{7,3},{8,4},{9,5},{1... | collective-permute-start | bytes 589832 | tf_op jit(solution)/shard_map/ppermute | solution.py:286
  111.7 0.2 collective-permute-start.15
  111.9 5.0 %collective-permute-start.25 = (f32[16,2048]{1,0:T(8,128)S(1)}, f32[16,2048]{1,0:T(8,128)S(1)}, u32[]{:S(2)}, u32[]{:S(2)}) collective-permute-start(f32[16,2048]{1,0:T(8,128)S(1)} %get-tuple-element.81), channel_id=1, source_target_pairs={{0,128},{16,144},{32,160},{48,176},{64,192},{80,208},{96,224},{112... | collective-permute-start | bytes 393224 | tf_op jit(solution)/shard_map/ppermute | solution.py:282
  116.9 0.2 collective-permute-start.26
  117.1 2.7 %collective-permute-done.15.refs_2_ = f32[192,256]{1,0:T(8,128)S(1)} collective-permute-done((f32[192,256]{1,0:T(8,128)S(1)}, f32[192,256]{1,0:T(8,128)S(1)}, u32[]{:S(2)}, u32[]{:S(2)}) %collective-permute-start.15) | collective-permute-done | bytes 196640 | tf_op jit(solution)/shard_map/ppermute | solution.py:286
  119.8 0.9 shard_map.89
  120.8 3.0 %collective-permute-done.25.refs_4_ = f32[16,2048]{1,0:T(8,128)S(1)} collective-permute-done((f32[16,2048]{1,0:T(8,128)S(1)}, f32[16,2048]{1,0:T(8,128)S(1)}, u32[]{:S(2)}, u32[]{:S(2)}) %collective-permute-start.25) | collective-permute-done | bytes 131104 | tf_op jit(solution)/shard_map/ppermute | solution.py:282
  123.8 3.0 %collective-permute-done.26.refs_5_ = f32[16,2048]{1,0:T(8,128)S(1)} collective-permute-done((f32[16,2048]{1,0:T(8,128)S(1)}, f32[16,2048]{1,0:T(8,128)S(1)}, u32[]{:S(2)}, u32[]{:S(2)}) %collective-permute-start.26) | collective-permute-done | bytes 131104 | tf_op jit(solution)/shard_map/ppermute | solution.py:282
  126.8 0.9 shard_map.95
  (54 shorter events, 0.7 us)
Async XLA Ops:
  0.6 2.7 %copy-start.9 = (f32[768]{0:T(1024)S(1)}, f32[768]{0:T(1024)}, u32[]{:S(2)}) copy-start(f32[768]{0:T(1024)} %param.11) | copy-start | bytes 9220
  0.6 3.0 %copy-start.8 = (f32[8192]{0:T(1024)S(1)}, f32[8192]{0:T(1024)}, u32[]{:S(2)}) copy-start(f32[8192]{0:T(1024)} %param.10) | copy-start | bytes 98308
  3.3 8.4 %collective-permute-start = (f32[2,768,256]{2,1,0:T(8,128)}, f32[2,768,256]{2,1,0:T(8,128)}, u32[]{:S(2)}, u32[]{:S(2)}) collective-permute-start(f32[2,768,256]{2,1,0:T(8,128)} %shard_map.77.refs_1_.refs_3_), channel_id=1, source_target_pairs={{0,16},{16,0},{32,48},{48,32},{64,80},{80,64},{96,112},{112,96},{1... | collective-permute-start | bytes 4718600 | tf_op jit(solution)/shard_map/ppermute | solution.py:282
  11.6 24.6 %copy-start = (bf16[768,4096]{1,0:T(8,128)(2,1)}, bf16[768,4096]{1,0:T(8,128)(2,1)S(1)}, u32[]{:S(2)}) copy-start(bf16[768,4096]{1,0:T(8,128)(2,1)S(1)} %get-tuple-element.47.refs_0_.refs_2_) | copy-start | bytes 18874372
  11.7 24.6 %copy-start.1 = (bf16[768,4096]{1,0:T(8,128)(2,1)}, bf16[768,4096]{1,0:T(8,128)(2,1)S(1)}, u32[]{:S(2)}) copy-start(bf16[768,4096]{1,0:T(8,128)(2,1)S(1)} %get-tuple-element.48.refs_1_.refs_3_) | copy-start | bytes 18874372
  19.0 10.9 %copy-start.2 = (bf16[768,4096]{1,0:T(8,128)(2,1)}, bf16[768,4096]{1,0:T(8,128)(2,1)S(1)}, u32[]{:S(2)}) copy-start(bf16[768,4096]{1,0:T(8,128)(2,1)S(1)} %get-tuple-element.50.refs_0_.refs_4_) | copy-start | bytes 18874372
  19.0 10.9 %copy-start.3 = (bf16[768,4096]{1,0:T(8,128)(2,1)}, bf16[768,4096]{1,0:T(8,128)(2,1)S(1)}, u32[]{:S(2)}) copy-start(bf16[768,4096]{1,0:T(8,128)(2,1)S(1)} %get-tuple-element.51.refs_1_.refs_5_) | copy-start | bytes 18874372
  19.0 1.4 %collective-permute-start.1 = (f32[8,768]{1,0:T(8,128)S(1)}, f32[8,768]{1,0:T(8,128)S(1)}, u32[]{:S(2)}, u32[]{:S(2)}) collective-permute-start(f32[8,768]{1,0:T(8,128)S(1)} %get-tuple-element.46.refs_0_), channel_id=1, source_target_pairs={{0,16},{16,0},{32,48},{48,32},{64,80},{80,64},{96,112},{112,96},{1... | collective-permute-start | bytes 73736 | tf_op jit(solution)/shard_map/ppermute | solution.py:282
  20.5 9.5 %collective-permute-start.4 = (f32[8,768]{1,0:T(8,128)S(1)}, f32[8,768]{1,0:T(8,128)S(1)}, u32[]{:S(2)}, u32[]{:S(2)}) collective-permute-start(f32[8,768]{1,0:T(8,128)S(1)} %shard_map.80.refs_0_.refs_5_), channel_id=1, source_target_pairs={{0,12},{1,13},{2,14},{3,15},{4,0},{5,1},{6,2},{7,3},{8,4},{9,5},{1... | collective-permute-start | bytes 73736 | tf_op jit(solution)/shard_map/ppermute | solution.py:286
  23.3 6.7 %collective-permute-start.3 = (f32[8,768]{1,0:T(8,128)S(1)}, f32[8,768]{1,0:T(8,128)S(1)}, u32[]{:S(2)}, u32[]{:S(2)}) collective-permute-start(f32[8,768]{1,0:T(8,128)S(1)} %shard_map.80.refs_0_.refs_5_), channel_id=1, source_target_pairs={{0,8},{1,9},{2,10},{3,11},{4,12},{5,13},{6,14},{7,15},{8,0},{9,1},... | collective-permute-start | bytes 73736 | tf_op jit(solution)/shard_map/ppermute | solution.py:286
  24.1 5.9 %collective-permute-start.2 = (f32[8,768]{1,0:T(8,128)S(1)}, f32[8,768]{1,0:T(8,128)S(1)}, u32[]{:S(2)}, u32[]{:S(2)}) collective-permute-start(f32[8,768]{1,0:T(8,128)S(1)} %shard_map.80.refs_0_.refs_5_), channel_id=1, source_target_pairs={{0,4},{1,5},{2,6},{3,7},{4,8},{5,9},{6,10},{7,11},{8,12},{9,13},{1... | collective-permute-start | bytes 73736 | tf_op jit(solution)/shard_map/ppermute | solution.py:286
  30.0 11.2 %collective-permute-start.7 = (f32[8,768]{1,0:T(8,128)S(1)}, f32[8,768]{1,0:T(8,128)S(1)}, u32[]{:S(2)}, u32[]{:S(2)}) collective-permute-start(f32[8,768]{1,0:T(8,128)S(1)} %shard_map.81.refs_5_.refs_0_), channel_id=1, source_target_pairs={{0,3},{1,0},{2,1},{3,2},{4,7},{5,4},{6,5},{7,6},{8,11},{9,8},{10,9... | collective-permute-start | bytes 73736 | tf_op jit(solution)/shard_map/ppermute | solution.py:286
  30.2 11.1 %collective-permute-start.6 = (f32[8,768]{1,0:T(8,128)S(1)}, f32[8,768]{1,0:T(8,128)S(1)}, u32[]{:S(2)}, u32[]{:S(2)}) collective-permute-start(f32[8,768]{1,0:T(8,128)S(1)} %shard_map.81.refs_5_.refs_0_), channel_id=1, source_target_pairs={{0,2},{1,3},{2,0},{3,1},{4,6},{5,7},{6,4},{7,5},{8,10},{9,11},{10,... | collective-permute-start | bytes 73736 | tf_op jit(solution)/shard_map/ppermute | solution.py:286
  33.5 7.8 %collective-permute-start.5 = (f32[8,768]{1,0:T(8,128)S(1)}, f32[8,768]{1,0:T(8,128)S(1)}, u32[]{:S(2)}, u32[]{:S(2)}) collective-permute-start(f32[8,768]{1,0:T(8,128)S(1)} %shard_map.81.refs_5_.refs_0_), channel_id=1, source_target_pairs={{0,1},{1,2},{2,3},{3,0},{4,5},{5,6},{6,7},{7,4},{8,9},{9,10},{10,1... | collective-permute-start | bytes 73736 | tf_op jit(solution)/shard_map/ppermute | solution.py:286
  41.2 1.5 %copy-start.6 = (f32[2,768,256]{2,1,0:T(8,128)}, f32[2,768,256]{2,1,0:T(8,128)S(1)}, u32[]{:S(2)}) copy-start(f32[2,768,256]{2,1,0:T(8,128)S(1)} %get-tuple-element.55.refs_2_) | copy-start | bytes 4718596
  42.8 1.1 copy-start.4
  43.9 12.4 %collective-permute-start.8 = (f32[768,256]{1,0:T(8,128)}, f32[768,256]{1,0:T(8,128)S(1)}, u32[]{:S(2)}, u32[]{:S(2)}) collective-permute-start(f32[768,256]{1,0:T(8,128)} %get-tuple-element.56), channel_id=1, source_target_pairs={{0,16},{16,0},{32,48},{48,32},{64,80},{80,64},{96,112},{112,96},{1... | collective-permute-start | bytes 2359304 | tf_op jit(solution)/shard_map/ppermute | solution.py:282
  43.9 1.4 %copy-start.5 = (bf16[256,3072]{1,0:T(8,128)(2,1)S(1)}, bf16[256,3072]{1,0:T(8,128)(2,1)}, u32[]{:S(2)}) copy-start(bf16[256,3072]{1,0:T(8,128)(2,1)} %copy-done.4) | copy-start | bytes 4718596
  45.3 11.0 %copy-start.7 = (f32[2,768,256]{2,1,0:T(8,128)S(1)}, f32[2,768,256]{2,1,0:T(8,128)}, u32[]{:S(2)}) copy-start(f32[2,768,256]{2,1,0:T(8,128)} %copy-done.6) | copy-start | bytes 4718596
  53.2 16.7 %collective-permute-start.19 = (f32[32,2048]{1,0:T(8,128)S(1)}, f32[32,2048]{1,0:T(8,128)S(1)}, u32[]{:S(2)}, u32[]{:S(2)}) collective-permute-start(f32[32,2048]{1,0:T(8,128)S(1)} %get-tuple-element.69), channel_id=1, source_target_pairs={{0,96},{16,112},{32,0},{48,16},{64,32},{80,48},{96,64},{112,80},{1... | collective-permute-start | bytes 786440 | tf_op jit(solution)/shard_map/ppermute | solution.py:282
  56.3 13.7 %collective-permute-start.18 = (f32[32,2048]{1,0:T(8,128)S(1)}, f32[32,2048]{1,0:T(8,128)S(1)}, u32[]{:S(2)}, u32[]{:S(2)}) collective-permute-start(f32[32,2048]{1,0:T(8,128)S(1)} %get-tuple-element.59.refs_4_), channel_id=1, source_target_pairs={{0,32},{16,48},{32,64},{48,80},{64,96},{80,112},{96,0},{112,16},{1... | collective-permute-start | bytes 786440 | tf_op jit(solution)/shard_map/ppermute | solution.py:282
  56.8 12.0 %collective-permute-start.9 = (f32[192,256]{1,0:T(8,128)S(1)}, f32[192,256]{1,0:T(8,128)S(1)}, u32[]{:S(2)}, u32[]{:S(2)}) collective-permute-start(f32[192,256]{1,0:T(8,128)S(1)} %get-tuple-element.61), channel_id=1, source_target_pairs={{0,4},{1,5},{2,6},{3,7},{4,8},{5,9},{6,10},{7,11},{8,12},{9,13},{1... | collective-permute-start | bytes 589832 | tf_op jit(solution)/shard_map/ppermute | solution.py:286
  58.7 10.1 %collective-permute-start.10 = (f32[192,256]{1,0:T(8,128)S(1)}, f32[192,256]{1,0:T(8,128)S(1)}, u32[]{:S(2)}, u32[]{:S(2)}) collective-permute-start(f32[192,256]{1,0:T(8,128)S(1)} %get-tuple-element.62), channel_id=1, source_target_pairs={{0,12},{1,13},{2,14},{3,15},{4,0},{5,1},{6,2},{7,3},{8,4},{9,5},{1... | collective-permute-start | bytes 589832 | tf_op jit(solution)/shard_map/ppermute | solution.py:286
  60.1 9.8 %collective-permute-start.11 = (f32[192,256]{1,0:T(8,128)S(1)}, f32[192,256]{1,0:T(8,128)S(1)}, u32[]{:S(2)}, u32[]{:S(2)}) collective-permute-start(f32[192,256]{1,0:T(8,128)S(1)} %get-tuple-element.63), channel_id=1, source_target_pairs={{0,8},{1,9},{2,10},{3,11},{4,12},{5,13},{6,14},{7,15},{8,0},{9,1},... | collective-permute-start | bytes 589832 | tf_op jit(solution)/shard_map/ppermute | solution.py:286
  70.1 21.5 %collective-permute-start.20 = (f32[96,2048]{1,0:T(8,128)S(1)}, f32[96,2048]{1,0:T(8,128)S(1)}, u32[]{:S(2)}, u32[]{:S(2)}) collective-permute-start(f32[96,2048]{1,0:T(8,128)S(1)} %get-tuple-element.70), channel_id=1, source_target_pairs={{0,32},{16,48},{32,64},{48,80},{64,96},{80,112},{96,0},{112,16},{1... | collective-permute-start | bytes 2359304 | tf_op jit(solution)/shard_map/ppermute | solution.py:282
  70.5 21.1 %collective-permute-start.21 = (f32[96,2048]{1,0:T(8,128)S(1)}, f32[96,2048]{1,0:T(8,128)S(1)}, u32[]{:S(2)}, u32[]{:S(2)}) collective-permute-start(f32[96,2048]{1,0:T(8,128)S(1)} %get-tuple-element.71), channel_id=1, source_target_pairs={{0,96},{16,112},{32,0},{48,16},{64,32},{80,48},{96,64},{112,80},{1... | collective-permute-start | bytes 2359304 | tf_op jit(solution)/shard_map/ppermute | solution.py:282
  73.4 15.9 %collective-permute-start.14 = (f32[192,256]{1,0:T(8,128)S(1)}, f32[192,256]{1,0:T(8,128)S(1)}, u32[]{:S(2)}, u32[]{:S(2)}) collective-permute-start(f32[192,256]{1,0:T(8,128)S(1)} %shard_map.87.refs_1_.refs_6_), channel_id=1, source_target_pairs={{0,3},{1,0},{2,1},{3,2},{4,7},{5,4},{6,5},{7,6},{8,11},{9,8},{10,9... | collective-permute-start | bytes 589832 | tf_op jit(solution)/shard_map/ppermute | solution.py:286
  73.4 15.9 %collective-permute-start.13 = (f32[192,256]{1,0:T(8,128)S(1)}, f32[192,256]{1,0:T(8,128)S(1)}, u32[]{:S(2)}, u32[]{:S(2)}) collective-permute-start(f32[192,256]{1,0:T(8,128)S(1)} %shard_map.87.refs_1_.refs_6_), channel_id=1, source_target_pairs={{0,2},{1,3},{2,0},{3,1},{4,6},{5,7},{6,4},{7,5},{8,10},{9,11},{10,... | collective-permute-start | bytes 589832 | tf_op jit(solution)/shard_map/ppermute | solution.py:286
  74.9 15.6 %collective-permute-start.12 = (f32[192,256]{1,0:T(8,128)S(1)}, f32[192,256]{1,0:T(8,128)S(1)}, u32[]{:S(2)}, u32[]{:S(2)}) collective-permute-start(f32[192,256]{1,0:T(8,128)S(1)} %shard_map.87.refs_1_.refs_6_), channel_id=1, source_target_pairs={{0,1},{1,2},{2,3},{3,0},{4,5},{5,6},{6,7},{7,4},{8,9},{9,10},{10,1... | collective-permute-start | bytes 589832 | tf_op jit(solution)/shard_map/ppermute | solution.py:286
  91.7 17.8 %collective-permute-start.24 = (f32[64,2048]{1,0:T(8,128)S(1)}, f32[64,2048]{1,0:T(8,128)S(1)}, u32[]{:S(2)}, u32[]{:S(2)}) collective-permute-start(f32[64,2048]{1,0:T(8,128)S(1)} %get-tuple-element.78), channel_id=1, source_target_pairs={{0,96},{16,112},{32,0},{48,16},{64,32},{80,48},{96,64},{112,80},{1... | collective-permute-start | bytes 1572872 | tf_op jit(solution)/shard_map/ppermute | solution.py:282
  93.4 16.2 %collective-permute-start.23 = (f32[64,2048]{1,0:T(8,128)S(1)}, f32[64,2048]{1,0:T(8,128)S(1)}, u32[]{:S(2)}, u32[]{:S(2)}) collective-permute-start(f32[64,2048]{1,0:T(8,128)S(1)} %get-tuple-element.74.refs_3_), channel_id=1, source_target_pairs={{0,32},{16,48},{32,64},{48,80},{64,96},{80,112},{96,0},{112,16},{1... | collective-permute-start | bytes 1572872 | tf_op jit(solution)/shard_map/ppermute | solution.py:282
  93.9 15.6 %collective-permute-start.22 = (f32[32,2048]{1,0:T(8,128)S(1)}, f32[32,2048]{1,0:T(8,128)S(1)}, u32[]{:S(2)}, u32[]{:S(2)}) collective-permute-start(f32[32,2048]{1,0:T(8,128)S(1)} %get-tuple-element.76), channel_id=1, source_target_pairs={{0,128},{16,144},{32,160},{48,176},{64,192},{80,208},{96,224},{112... | collective-permute-start | bytes 786440 | tf_op jit(solution)/shard_map/ppermute | solution.py:282
  98.8 18.1 %collective-permute-start.17 = (f32[192,256]{1,0:T(8,128)S(1)}, f32[192,256]{1,0:T(8,128)S(1)}, u32[]{:S(2)}, u32[]{:S(2)}) collective-permute-start(f32[192,256]{1,0:T(8,128)S(1)} %shard_map.88.refs_1_.refs_4_), channel_id=1, source_target_pairs={{0,8},{1,9},{2,10},{3,11},{4,12},{5,13},{6,14},{7,15},{8,0},{9,1},... | collective-permute-start | bytes 589832 | tf_op jit(solution)/shard_map/ppermute | solution.py:286
  109.7 17.1 %collective-permute-start.27 = (f32[16,4096]{1,0:T(8,128)S(1)}, f32[16,4096]{1,0:T(8,128)S(1)}, u32[]{:S(2)}, u32[]{:S(2)}) collective-permute-start(f32[16,4096]{1,0:T(8,128)S(1)} %get-tuple-element.83), channel_id=1, source_target_pairs={{0,16},{16,0},{32,48},{48,32},{64,80},{80,64},{96,112},{112,96},{1... | collective-permute-start | bytes 786440 | tf_op jit(solution)/shard_map/ppermute | solution.py:282
  109.8 7.3 %collective-permute-start.16 = (f32[192,256]{1,0:T(8,128)S(1)}, f32[192,256]{1,0:T(8,128)S(1)}, u32[]{:S(2)}, u32[]{:S(2)}) collective-permute-start(f32[192,256]{1,0:T(8,128)S(1)} %shard_map.88.refs_1_.refs_4_), channel_id=1, source_target_pairs={{0,12},{1,13},{2,14},{3,15},{4,0},{5,1},{6,2},{7,3},{8,4},{9,5},{1... | collective-permute-start | bytes 589832 | tf_op jit(solution)/shard_map/ppermute | solution.py:286
  111.7 8.2 %collective-permute-start.15 = (f32[192,256]{1,0:T(8,128)S(1)}, f32[192,256]{1,0:T(8,128)S(1)}, u32[]{:S(2)}, u32[]{:S(2)}) collective-permute-start(f32[192,256]{1,0:T(8,128)S(1)} %shard_map.88.refs_1_.refs_4_), channel_id=1, source_target_pairs={{0,4},{1,5},{2,6},{3,7},{4,8},{5,9},{6,10},{7,11},{8,12},{9,13},{1... | collective-permute-start | bytes 589832 | tf_op jit(solution)/shard_map/ppermute | solution.py:286
  111.9 11.9 %collective-permute-start.25 = (f32[16,2048]{1,0:T(8,128)S(1)}, f32[16,2048]{1,0:T(8,128)S(1)}, u32[]{:S(2)}, u32[]{:S(2)}) collective-permute-start(f32[16,2048]{1,0:T(8,128)S(1)} %get-tuple-element.81), channel_id=1, source_target_pairs={{0,128},{16,144},{32,160},{48,176},{64,192},{80,208},{96,224},{112... | collective-permute-start | bytes 393224 | tf_op jit(solution)/shard_map/ppermute | solution.py:282
  116.9 9.9 %collective-permute-start.26 = (f32[16,2048]{1,0:T(8,128)S(1)}, f32[16,2048]{1,0:T(8,128)S(1)}, u32[]{:S(2)}, u32[]{:S(2)}) collective-permute-start(f32[16,2048]{1,0:T(8,128)S(1)} %get-tuple-element.82), channel_id=1, source_target_pairs={{0,144},{16,128},{32,176},{48,160},{64,208},{80,192},{96,240},{112... | collective-permute-start | bytes 393224 | tf_op jit(solution)/shard_map/ppermute | solution.py:282

commit v3 on v2

--- a/solution.py
+++ b/solution.py
@@ -246,8 +246,12 @@
     out_ref[...] = a_ref[...] + b_ref[...] + c_ref[...] + d_ref[...]
 
 
-def rows_kernel(x_ref, a_ref, b_ref, c_ref, d_ref, rows_ref, out_ref):
-    total = a_ref[...] + b_ref[...] + c_ref[...] + d_ref[...]
+def add2_kernel(a_ref, b_ref, out_ref):
+    out_ref[...] = a_ref[...] + b_ref[...]
+
+
+def rows_kernel(x_ref, a_ref, b_ref, rows_ref, out_ref):
+    total = a_ref[...] + b_ref[...]
     v = rows_ref[...].astype(F32)
     norm = jnp.sqrt(jnp.sum(v * v, axis=1, keepdims=True) + norm_eps)
     z = v / norm
@@ -280,6 +284,10 @@
 
 def to_dp(v, pairs):
     return lax.ppermute(v, "dp", pairs)
+
+
+def swap_z(v, bit):
+    return lax.ppermute(v, "mp", [(i, i ^ bit) for i in range(16)])
 
 
 def to_mp(v, dx, dz):
@@ -381,9 +389,10 @@
     mp, mm = call(ring_kernel, (shape((96, w0)),) * 2, bp0, bm0, ap1, am1, to_dp(ap0, YP), to_dp(am0, YM),
                   after=(part,), in_specs=[VM] * 6, out_specs=[VM] * 2)
     gp, gm = to_dp(mp, YP), to_dp(mm, YM)
+    pair = call(add2_kernel, quarter, part, swap_z(part, 1), **small)
     fixed = pl.BlockSpec((rows // 4, feats), lambda i, c: (0, 0))
-    mine = call(rows_kernel, quarter, x_s, part, *[to_mp(part, 0, k) for k in (1, 2, 3)], hbm(student_rows),
-                scalars=1, grid=(1,), in_specs=[fixed] * 4 + [pl.BlockSpec((rows // 4, feats), lambda i, c: (c[0], 0))],
+    mine = call(rows_kernel, quarter, x_s, pair, swap_z(pair, 2), hbm(student_rows),
+                scalars=1, grid=(1,), in_specs=[fixed] * 2 + [pl.BlockSpec((rows // 4, feats), lambda i, c: (c[0], 0))],
                 out_specs=fixed)
     bp1, bm1 = call(ring_last_kernel, (shape((64, w1)),) * 2, bp1, bm1, gp, gm, after=(mine,),
                     in_specs=[VM] * 4, out_specs=[VM] * 2)

time: 130 us -> 129 us (level)
  starting transfers between devices: 41.7 us -> 39.8 us
  waiting for transfers between devices: 33 us -> 34.8 us
    ppermute x15 -> x12, waiting for transfers between devices: 17.1 us -> 3.9 us  [to_mp(): return lax.ppermute(v, 'mp', mp_pairs(dx, dz))]
    ppermute x0 -> x2, waiting for transfers between devices: none -> 12.2 us  [swap_z(): return lax.ppermute(v, 'mp', [(i, i ^ bit) for i in range(16)])]
    ppermute x15 -> x12, starting transfers between devices: 22.5 us -> 18.7 us  [to_mp(): return lax.ppermute(v, 'mp', mp_pairs(dx, dz))]
    ppermute x13, waiting for transfers between devices: 15.8 us -> 18.7 us  [to_dp(): return lax.ppermute(v, 'dp', pairs)]
    pallas_call x19 -> x20, Pallas kernels: 49 us -> 49 us  [call(): pl.pallas_call(body, out_shape=out, grid_spec=pltpu.PrefetchScalarGridSpe...]
  transfers between devices with their start and end apart: 28 -> 27, of which waited for: 8 -> 9; matrix products, arithmetic and copies ran while one was open for 0% -> 0% of each run, Pallas kernels for 29% -> 29%
where the time goes in v3:
time: 129 us; the launch traced here: 127 us
  Pallas kernels  49 us (38%)
  starting transfers between devices  39.8 us (31%)
  waiting for transfers between devices  34.8 us (27%)
  local copies, waits for them, and re-layouts  2.85 us (2%)
    pallas_call x20, Pallas kernels, call(): pl.pallas_call(body, out_shape=out, grid_spec=pltpu.PrefetchScalarGridSpe...  49 us
    ppermute x13, starting transfers between devices, to_dp(): return lax.ppermute(v, 'dp', pairs)  19.9 us
    ppermute x12, starting transfers between devices, to_mp(): return lax.ppermute(v, 'mp', mp_pairs(dx, dz))  18.7 us
    ppermute x13, waiting for transfers between devices, to_dp(): return lax.ppermute(v, 'dp', pairs)  18.7 us
    ppermute x2, waiting for transfers between devices, swap_z(): return lax.ppermute(v, 'mp', [(i, i ^ bit) for i in range(16)])  12.2 us
    ppermute x12, waiting for transfers between devices, to_mp(): return lax.ppermute(v, 'mp', mp_pairs(dx, dz))  3.9 us
    unnamed x20, local copies, waits for them, and re-layouts  2.59 us
  transfers between devices with their start and end apart: 27, of which 9 were waited for; matrix products, arithmetic and copies ran while one was open for 0% of the time, Pallas kernels for 29%

profile of v3, /device:TPU:32, one launch (start us, length us, event | category | flops | bytes accessed | tf_op | source)
XLA Modules:
  0.0 127.5 jit_solution(15805021548566509732)
XLA Ops:
  0.7 2.7 %shard_map.77.refs_1_.refs_3_ = f32[2,768,256]{2,1,0:T(8,128)} custom-call(bf16[768,256]{1,0:T(8,128)(2,1)} %refs_3_.3, bf16[768,256]{1,0:T(8,128)(2,1)} %refs_1_.1), custom_call_target="tpu_custom_call" | custom-call | bytes 3145728 | tf_op jit(solution)/shard_map/pallas_call | solution.py:30
  3.3 0.1 stack.67.refs_0_
  3.6 8.0 %shard_map.78 = (bf16[768,4096]{1,0:T(8,128)(2,1)S(1)}, bf16[768,4096]{1,0:T(8,128)(2,1)S(1)}, bf16[256,4096]{1,0:T(8,128)(2,1)S(1)}, bf16[256,4096]{1,0:T(8,128...) custom-call(s32[1]{0:T(128)} %bitcast.1.refs_0_, f32[2,768,256]{2,1,0:T(8,128)} %shard_map.77.refs_1_.refs_3_, ...), custom_call_target="tpu_custom_call" | custom-call | flops 3221225472 | bytes 8388608 | tf_op jit(solution)/shard_map/pallas_call | solution.py:30
  11.7 7.3 %shard_map.79 = (bf16[768,4096]{1,0:T(8,128)(2,1)S(1)}, bf16[768,4096]{1,0:T(8,128)(2,1)S(1)}, f32[8,768]{1,0:T(8,128)S(1)}) custom-call(s32[1]{0:T(128)} %bitcast.1.refs_0_, f32[2,768,256]{2,1,0:T(8,128)} %collective-permute-done.refs_1_.refs_3_, bf16[256,4096]{1,0:T(8,128)(2,1)S(1)} %get-tuple-element.43.refs_2_.refs_6_, ...), custom_call_target="tpu_custom_call" | custom-call | flops 3221225472 | bytes 8388608 | tf_op jit(solution)/shard_map/pallas_call | solution.py:30
  19.0 0.6 collective-permute-start.1
  19.6 0.1 fusion.refs_4_
  19.7 0.7 collective-permute-done.1.refs_1_
  20.5 2.8 %collective-permute-start.4 = (f32[8,768]{1,0:T(8,128)S(1)}, f32[8,768]{1,0:T(8,128)S(1)}, u32[]{:S(2)}, u32[]{:S(2)}) collective-permute-start(f32[8,768]{1,0:T(8,128)S(1)} %shard_map.80.refs_0_.refs_5_), channel_id=1, source_target_pairs={{0,12},{1,13},{2,14},{3,15},{4,0},{5,1},{6,2},{7,3},{8,4},{9,5},{1... | collective-permute-start | bytes 73736 | tf_op jit(solution)/shard_map/ppermute | solution.py:294
  23.3 0.8 collective-permute-start.3
  24.1 0.9 collective-permute-start.2
  25.0 4.9 %shard_map.83 = (f32[2,768,256]{2,1,0:T(8,128)S(1)}, bf16[256,768]{1,0:T(8,128)(2,1)S(1)}) custom-call(bf16[768,4096]{1,0:T(8,128)(2,1)S(1)} %get-tuple-element.50.refs_0_.refs_4_, bf16[768,4096]{1,0:T(8,128)(2,1)S(1)} %get-tuple-element.51.refs_1_.refs_5_, bf16[256,4096]{1,0:T(8,128)(2,1)S(1)} %get-tuple-element.43.refs_2_.refs_6_, ...), custom_call_target="tpu_custom_call" | custom-call | flops 3221225472 | bytes 8388608 | tf_op jit(solution)/shard_map/pallas_call | solution.py:30
  30.0 0.2 collective-permute-start.7
  30.2 3.3 %collective-permute-start.6 = (f32[8,768]{1,0:T(8,128)S(1)}, f32[8,768]{1,0:T(8,128)S(1)}, u32[]{:S(2)}, u32[]{:S(2)}) collective-permute-start(f32[8,768]{1,0:T(8,128)S(1)} %shard_map.81.refs_5_.refs_0_), channel_id=1, source_target_pairs={{0,2},{1,3},{2,0},{3,1},{4,6},{5,7},{6,4},{7,5},{8,10},{9,11},{10,... | collective-permute-start | bytes 73736 | tf_op jit(solution)/shard_map/ppermute | solution.py:294
  33.5 2.8 %collective-permute-start.5 = (f32[8,768]{1,0:T(8,128)S(1)}, f32[8,768]{1,0:T(8,128)S(1)}, u32[]{:S(2)}, u32[]{:S(2)}) collective-permute-start(f32[8,768]{1,0:T(8,128)S(1)} %shard_map.81.refs_5_.refs_0_), channel_id=1, source_target_pairs={{0,1},{1,2},{2,3},{3,0},{4,5},{5,6},{6,7},{7,4},{8,9},{9,10},{10,1... | collective-permute-start | bytes 73736 | tf_op jit(solution)/shard_map/ppermute | solution.py:294
  36.3 4.9 %shard_map.82 = (f32[2,768,256]{2,1,0:T(8,128)S(1)}, bf16[256,768]{1,0:T(8,128)(2,1)S(1)}) custom-call(bf16[768,4096]{1,0:T(8,128)(2,1)S(1)} %get-tuple-element.47.refs_0_.refs_2_, bf16[768,4096]{1,0:T(8,128)(2,1)S(1)} %get-tuple-element.48.refs_1_.refs_3_, bf16[256,4096]{1,0:T(8,128)(2,1)S(1)} %get-tuple-element.43.refs_2_.refs_6_, ...), custom_call_target="tpu_custom_call" | custom-call | flops 3221225472 | bytes 8388608 | tf_op jit(solution)/shard_map/pallas_call | solution.py:30
  41.3 1.5 %shard_map.84 = (bf16[256,3072]{1,0:T(8,128)(2,1)S(1)}, f32[4,768]{1,0:T(4,128)S(1)}, f32[768,256]{1,0:T(8,128)}) custom-call(f32[8,768]{1,0:T(8,128)S(1)} %shard_map.81.refs_5_.refs_0_, f32[8,768]{1,0:T(8,128)S(1)} %collective-permute-done.5.refs_1_, f32[8,768]{1,0:T(8,128)S(1)} %collective-permute-done.6.refs_2_, ...), custom_call_target="tpu_custom_call" | custom-call | tf_op jit(solution)/shard_map/pallas_call | solution.py:30
  42.8 1.1 copy-done.4
  44.0 1.4 %copy-done.5 = bf16[256,3072]{1,0:T(8,128)(2,1)S(1)} copy-done((bf16[256,3072]{1,0:T(8,128)(2,1)S(1)}, bf16[256,3072]{1,0:T(8,128)(2,1)}, u32[]{:S(2)}) %copy-start.5) | copy-done | bytes 1572888
  45.4 7.9 %shard_map.85 = (f32[64,2048]{1,0:T(8,128)S(1)}, f32[64,2048]{1,0:T(8,128)S(1)}, f32[64,2048]{1,0:T(8,128)S(1)}, f32[32,2048]{1,0:T(8,128)S(1)}, f32[32,2048]{1,0:T(8,128)S(1)}) custom-call(s32[16]{0:T(128)S(1)} %stack.67.refs_0_, bf16[256,3072]{1,0:T(8,128)(2,1)S(1)} %copy-done.5, bf16[768,4096]{1,0:T(8,128)(2,1)} %copy-done, bf16[768,4096]{1,0:T(8,128)(2,1)} %copy-done.1, ...), custom_call_target="tpu_custom_call" | custom-call | flops 3221225472 | bytes 13631488 | tf_op jit(solution)/shard_map/pallas_call | solution.py:30
  53.3 3.1 %collective-permute-start.18 = (f32[32,2048]{1,0:T(8,128)S(1)}, f32[32,2048]{1,0:T(8,128)S(1)}, u32[]{:S(2)}, u32[]{:S(2)}) collective-permute-start(f32[32,2048]{1,0:T(8,128)S(1)} %get-tuple-element.69), channel_id=1, source_target_pairs={{0,96},{16,112},{32,0},{48,16},{64,32},{80,48},{96,64},{112,80},{1... | collective-permute-start | bytes 786440 | tf_op jit(solution)/shard_map/ppermute | solution.py:286
  56.4 0.5 shard_map.86
  56.8 1.9 %collective-permute-start.9 = (f32[192,256]{1,0:T(8,128)S(1)}, f32[192,256]{1,0:T(8,128)S(1)}, u32[]{:S(2)}, u32[]{:S(2)}) collective-permute-start(f32[192,256]{1,0:T(8,128)S(1)} %get-tuple-element.61), channel_id=1, source_target_pairs={{0,4},{1,5},{2,6},{3,7},{4,8},{5,9},{6,10},{7,11},{8,12},{9,13},{1... | collective-permute-start | bytes 589832 | tf_op jit(solution)/shard_map/ppermute | solution.py:294
  58.7 1.4 %collective-permute-start.10 = (f32[192,256]{1,0:T(8,128)S(1)}, f32[192,256]{1,0:T(8,128)S(1)}, u32[]{:S(2)}, u32[]{:S(2)}) collective-permute-start(f32[192,256]{1,0:T(8,128)S(1)} %get-tuple-element.62), channel_id=1, source_target_pairs={{0,12},{1,13},{2,14},{3,15},{4,0},{5,1},{6,2},{7,3},{8,4},{9,5},{1... | collective-permute-start | bytes 589832 | tf_op jit(solution)/shard_map/ppermute | solution.py:294
  60.1 0.7 collective-permute-start.11
  60.9 7.9 %shard_map.91 = (f32[64,2048]{1,0:T(8,128)S(1)}, f32[64,2048]{1,0:T(8,128)S(1)}, f32[64,2048]{1,0:T(8,128)S(1)}, f32[32,2048]{1,0:T(8,128)S(1)}, f32[32,2048]{1,0:T(8,128)S(1)}) custom-call(s32[16]{0:T(128)S(1)} %stack.67.refs_0_, bf16[256,3072]{1,0:T(8,128)(2,1)S(1)} %copy-done.5, bf16[768,4096]{1,0:T(8,128)(2,1)} %copy-done, bf16[768,4096]{1,0:T(8,128)(2,1)} %copy-done.1, ...), custom_call_target="tpu_custom_call" | custom-call | flops 3221225472 | bytes 13631488 | tf_op jit(solution)/shard_map/pallas_call | solution.py:30
  68.8 1.1 collective-permute-done.11.refs_3_
  70.0 0.1 shard_map.92
  70.1 0.4 collective-permute-start.19
  70.5 2.9 %collective-permute-start.20 = (f32[96,2048]{1,0:T(8,128)S(1)}, f32[96,2048]{1,0:T(8,128)S(1)}, u32[]{:S(2)}, u32[]{:S(2)}) collective-permute-start(f32[96,2048]{1,0:T(8,128)S(1)} %get-tuple-element.71), channel_id=1, source_target_pairs={{0,96},{16,112},{32,0},{48,16},{64,32},{80,48},{96,64},{112,80},{1... | collective-permute-start | bytes 2359304 | tf_op jit(solution)/shard_map/ppermute | solution.py:286
  73.4 5.7 %collective-permute-done.12.refs_1_ = f32[192,256]{1,0:T(8,128)S(1)} collective-permute-done((f32[192,256]{1,0:T(8,128)S(1)}, f32[192,256]{1,0:T(8,128)S(1)}, u32[]{:S(2)}, u32[]{:S(2)}) %collective-permute-start.12) | collective-permute-done | bytes 196640 | tf_op jit(solution)/shard_map/ppermute | solution.py:290
  79.1 1.2 collective-permute-start.13
  80.3 6.5 %collective-permute-done.13.refs_2_ = f32[192,256]{1,0:T(8,128)S(1)} collective-permute-done((f32[192,256]{1,0:T(8,128)S(1)}, f32[192,256]{1,0:T(8,128)S(1)}, u32[]{:S(2)}, u32[]{:S(2)}) %collective-permute-start.13) | collective-permute-done | bytes 196640 | tf_op jit(solution)/shard_map/ppermute | solution.py:290
  86.9 1.1 shard_map.89.refs_1_.refs_4_
  88.0 2.3 %collective-permute-done.19.refs_2_.refs_1_ = f32[96,2048]{1,0:T(8,128)S(1)} collective-permute-done((f32[96,2048]{1,0:T(8,128)S(1)}, f32[96,2048]{1,0:T(8,128)S(1)}, u32[]{:S(2)}, u32[]{:S(2)}) %collective-permute-start.19) | collective-permute-done | bytes 786464 | tf_op jit(solution)/shard_map/ppermute | solution.py:286
  90.4 3.0 %collective-permute-start.23 = (f32[64,2048]{1,0:T(8,128)S(1)}, f32[64,2048]{1,0:T(8,128)S(1)}, u32[]{:S(2)}, u32[]{:S(2)}) collective-permute-start(f32[64,2048]{1,0:T(8,128)S(1)} %get-tuple-element.78), channel_id=1, source_target_pairs={{0,96},{16,112},{32,0},{48,16},{64,32},{80,48},{96,64},{112,80},{1... | collective-permute-start | bytes 1572872 | tf_op jit(solution)/shard_map/ppermute | solution.py:286
  93.5 4.6 %collective-permute-start.21 = (f32[32,2048]{1,0:T(8,128)S(1)}, f32[32,2048]{1,0:T(8,128)S(1)}, u32[]{:S(2)}, u32[]{:S(2)}) collective-permute-start(f32[32,2048]{1,0:T(8,128)S(1)} %get-tuple-element.76), channel_id=1, source_target_pairs={{0,128},{16,144},{32,160},{48,176},{64,192},{80,208},{96,224},{112... | collective-permute-start | bytes 786440 | tf_op jit(solution)/shard_map/ppermute | solution.py:286
  98.1 1.7 %collective-permute-start.16 = (f32[192,256]{1,0:T(8,128)S(1)}, f32[192,256]{1,0:T(8,128)S(1)}, u32[]{:S(2)}, u32[]{:S(2)}) collective-permute-start(f32[192,256]{1,0:T(8,128)S(1)} %shard_map.89.refs_1_.refs_4_), channel_id=1, source_target_pairs={{0,8},{1,9},{2,10},{3,11},{4,12},{5,13},{6,14},{7,15},{8,0},{9,1},... | collective-permute-start | bytes 589832 | tf_op jit(solution)/shard_map/ppermute | solution.py:294
  99.8 9.5 %collective-permute-done.21.refs_4_.refs_2_ = f32[32,2048]{1,0:T(8,128)S(1)} collective-permute-done((f32[32,2048]{1,0:T(8,128)S(1)}, f32[32,2048]{1,0:T(8,128)S(1)}, u32[]{:S(2)}, u32[]{:S(2)}) %collective-permute-start.21) | collective-permute-done | bytes 262176 | tf_op jit(solution)/shard_map/ppermute | solution.py:286
  109.4 0.1 collective-permute-start.26
  109.5 1.9 %collective-permute-start.15 = (f32[192,256]{1,0:T(8,128)S(1)}, f32[192,256]{1,0:T(8,128)S(1)}, u32[]{:S(2)}, u32[]{:S(2)}) collective-permute-start(f32[192,256]{1,0:T(8,128)S(1)} %shard_map.89.refs_1_.refs_4_), channel_id=1, source_target_pairs={{0,12},{1,13},{2,14},{3,15},{4,0},{5,1},{6,2},{7,3},{8,4},{9,5},{1... | collective-permute-start | bytes 589832 | tf_op jit(solution)/shard_map/ppermute | solution.py:294
  111.3 0.2 collective-permute-start.14
  111.6 4.5 %collective-permute-start.24 = (f32[16,2048]{1,0:T(8,128)S(1)}, f32[16,2048]{1,0:T(8,128)S(1)}, u32[]{:S(2)}, u32[]{:S(2)}) collective-permute-start(f32[16,2048]{1,0:T(8,128)S(1)} %get-tuple-element.81), channel_id=1, source_target_pairs={{0,128},{16,144},{32,160},{48,176},{64,192},{80,208},{96,224},{112... | collective-permute-start | bytes 393224 | tf_op jit(solution)/shard_map/ppermute | solution.py:286
  116.0 0.7 collective-permute-start.25
  116.8 2.7 %collective-permute-done.14.refs_2_ = f32[192,256]{1,0:T(8,128)S(1)} collective-permute-done((f32[192,256]{1,0:T(8,128)S(1)}, f32[192,256]{1,0:T(8,128)S(1)}, u32[]{:S(2)}, u32[]{:S(2)}) %collective-permute-start.14) | collective-permute-done | bytes 196640 | tf_op jit(solution)/shard_map/ppermute | solution.py:294
  119.5 0.9 shard_map.90
  120.4 3.2 %collective-permute-done.24.refs_4_ = f32[16,2048]{1,0:T(8,128)S(1)} collective-permute-done((f32[16,2048]{1,0:T(8,128)S(1)}, f32[16,2048]{1,0:T(8,128)S(1)}, u32[]{:S(2)}, u32[]{:S(2)}) %collective-permute-start.24) | collective-permute-done | bytes 131104 | tf_op jit(solution)/shard_map/ppermute | solution.py:286
  123.6 3.0 %collective-permute-done.25.refs_5_ = f32[16,2048]{1,0:T(8,128)S(1)} collective-permute-done((f32[16,2048]{1,0:T(8,128)S(1)}, f32[16,2048]{1,0:T(8,128)S(1)}, u32[]{:S(2)}, u32[]{:S(2)}) %collective-permute-start.25) | collective-permute-done | bytes 131104 | tf_op jit(solution)/shard_map/ppermute | solution.py:286
  126.6 0.9 shard_map.96
  (53 shorter events, 0.6 us)
Async XLA Ops:
  0.6 2.7 %copy-start.9 = (f32[768]{0:T(1024)S(1)}, f32[768]{0:T(1024)}, u32[]{:S(2)}) copy-start(f32[768]{0:T(1024)} %param.11) | copy-start | bytes 9220
  0.6 3.0 %copy-start.8 = (f32[8192]{0:T(1024)S(1)}, f32[8192]{0:T(1024)}, u32[]{:S(2)}) copy-start(f32[8192]{0:T(1024)} %param.10) | copy-start | bytes 98308
  3.3 8.4 %collective-permute-start = (f32[2,768,256]{2,1,0:T(8,128)}, f32[2,768,256]{2,1,0:T(8,128)}, u32[]{:S(2)}, u32[]{:S(2)}) collective-permute-start(f32[2,768,256]{2,1,0:T(8,128)} %shard_map.77.refs_1_.refs_3_), channel_id=1, source_target_pairs={{0,16},{16,0},{32,48},{48,32},{64,80},{80,64},{96,112},{112,96},{1... | collective-permute-start | bytes 4718600 | tf_op jit(solution)/shard_map/ppermute | solution.py:286
  11.7 24.6 %copy-start = (bf16[768,4096]{1,0:T(8,128)(2,1)}, bf16[768,4096]{1,0:T(8,128)(2,1)S(1)}, u32[]{:S(2)}) copy-start(bf16[768,4096]{1,0:T(8,128)(2,1)S(1)} %get-tuple-element.47.refs_0_.refs_2_) | copy-start | bytes 18874372
  11.7 24.6 %copy-start.1 = (bf16[768,4096]{1,0:T(8,128)(2,1)}, bf16[768,4096]{1,0:T(8,128)(2,1)S(1)}, u32[]{:S(2)}) copy-start(bf16[768,4096]{1,0:T(8,128)(2,1)S(1)} %get-tuple-element.48.refs_1_.refs_3_) | copy-start | bytes 18874372
  19.0 10.9 %copy-start.2 = (bf16[768,4096]{1,0:T(8,128)(2,1)}, bf16[768,4096]{1,0:T(8,128)(2,1)S(1)}, u32[]{:S(2)}) copy-start(bf16[768,4096]{1,0:T(8,128)(2,1)S(1)} %get-tuple-element.50.refs_0_.refs_4_) | copy-start | bytes 18874372
  19.0 10.9 %copy-start.3 = (bf16[768,4096]{1,0:T(8,128)(2,1)}, bf16[768,4096]{1,0:T(8,128)(2,1)S(1)}, u32[]{:S(2)}) copy-start(bf16[768,4096]{1,0:T(8,128)(2,1)S(1)} %get-tuple-element.51.refs_1_.refs_5_) | copy-start | bytes 18874372
  19.0 1.4 %collective-permute-start.1 = (f32[8,768]{1,0:T(8,128)S(1)}, f32[8,768]{1,0:T(8,128)S(1)}, u32[]{:S(2)}, u32[]{:S(2)}) collective-permute-start(f32[8,768]{1,0:T(8,128)S(1)} %get-tuple-element.46.refs_0_), channel_id=1, source_target_pairs={{0,16},{16,0},{32,48},{48,32},{64,80},{80,64},{96,112},{112,96},{1... | collective-permute-start | bytes 73736 | tf_op jit(solution)/shard_map/ppermute | solution.py:286
  20.5 9.5 %collective-permute-start.4 = (f32[8,768]{1,0:T(8,128)S(1)}, f32[8,768]{1,0:T(8,128)S(1)}, u32[]{:S(2)}, u32[]{:S(2)}) collective-permute-start(f32[8,768]{1,0:T(8,128)S(1)} %shard_map.80.refs_0_.refs_5_), channel_id=1, source_target_pairs={{0,12},{1,13},{2,14},{3,15},{4,0},{5,1},{6,2},{7,3},{8,4},{9,5},{1... | collective-permute-start | bytes 73736 | tf_op jit(solution)/shard_map/ppermute | solution.py:294
  23.3 6.7 %collective-permute-start.3 = (f32[8,768]{1,0:T(8,128)S(1)}, f32[8,768]{1,0:T(8,128)S(1)}, u32[]{:S(2)}, u32[]{:S(2)}) collective-permute-start(f32[8,768]{1,0:T(8,128)S(1)} %shard_map.80.refs_0_.refs_5_), channel_id=1, source_target_pairs={{0,8},{1,9},{2,10},{3,11},{4,12},{5,13},{6,14},{7,15},{8,0},{9,1},... | collective-permute-start | bytes 73736 | tf_op jit(solution)/shard_map/ppermute | solution.py:294
  24.1 5.9 %collective-permute-start.2 = (f32[8,768]{1,0:T(8,128)S(1)}, f32[8,768]{1,0:T(8,128)S(1)}, u32[]{:S(2)}, u32[]{:S(2)}) collective-permute-start(f32[8,768]{1,0:T(8,128)S(1)} %shard_map.80.refs_0_.refs_5_), channel_id=1, source_target_pairs={{0,4},{1,5},{2,6},{3,7},{4,8},{5,9},{6,10},{7,11},{8,12},{9,13},{1... | collective-permute-start | bytes 73736 | tf_op jit(solution)/shard_map/ppermute | solution.py:294
  30.0 11.3 %collective-permute-start.7 = (f32[8,768]{1,0:T(8,128)S(1)}, f32[8,768]{1,0:T(8,128)S(1)}, u32[]{:S(2)}, u32[]{:S(2)}) collective-permute-start(f32[8,768]{1,0:T(8,128)S(1)} %shard_map.81.refs_5_.refs_0_), channel_id=1, source_target_pairs={{0,3},{1,0},{2,1},{3,2},{4,7},{5,4},{6,5},{7,6},{8,11},{9,8},{10,9... | collective-permute-start | bytes 73736 | tf_op jit(solution)/shard_map/ppermute | solution.py:294
  30.2 11.1 %collective-permute-start.6 = (f32[8,768]{1,0:T(8,128)S(1)}, f32[8,768]{1,0:T(8,128)S(1)}, u32[]{:S(2)}, u32[]{:S(2)}) collective-permute-start(f32[8,768]{1,0:T(8,128)S(1)} %shard_map.81.refs_5_.refs_0_), channel_id=1, source_target_pairs={{0,2},{1,3},{2,0},{3,1},{4,6},{5,7},{6,4},{7,5},{8,10},{9,11},{10,... | collective-permute-start | bytes 73736 | tf_op jit(solution)/shard_map/ppermute | solution.py:294
  33.5 7.8 %collective-permute-start.5 = (f32[8,768]{1,0:T(8,128)S(1)}, f32[8,768]{1,0:T(8,128)S(1)}, u32[]{:S(2)}, u32[]{:S(2)}) collective-permute-start(f32[8,768]{1,0:T(8,128)S(1)} %shard_map.81.refs_5_.refs_0_), channel_id=1, source_target_pairs={{0,1},{1,2},{2,3},{3,0},{4,5},{5,6},{6,7},{7,4},{8,9},{9,10},{10,1... | collective-permute-start | bytes 73736 | tf_op jit(solution)/shard_map/ppermute | solution.py:294
  41.3 1.5 %copy-start.6 = (f32[2,768,256]{2,1,0:T(8,128)}, f32[2,768,256]{2,1,0:T(8,128)S(1)}, u32[]{:S(2)}) copy-start(f32[2,768,256]{2,1,0:T(8,128)S(1)} %get-tuple-element.55.refs_2_) | copy-start | bytes 4718596
  42.8 1.2 copy-start.4
  43.9 12.4 %collective-permute-start.8 = (f32[768,256]{1,0:T(8,128)}, f32[768,256]{1,0:T(8,128)S(1)}, u32[]{:S(2)}, u32[]{:S(2)}) collective-permute-start(f32[768,256]{1,0:T(8,128)} %get-tuple-element.56), channel_id=1, source_target_pairs={{0,16},{16,0},{32,48},{48,32},{64,80},{80,64},{96,112},{112,96},{1... | collective-permute-start | bytes 2359304 | tf_op jit(solution)/shard_map/ppermute | solution.py:286
  44.0 1.4 %copy-start.5 = (bf16[256,3072]{1,0:T(8,128)(2,1)S(1)}, bf16[256,3072]{1,0:T(8,128)(2,1)}, u32[]{:S(2)}) copy-start(bf16[256,3072]{1,0:T(8,128)(2,1)} %copy-done.4) | copy-start | bytes 4718596
  45.4 11.0 %copy-start.7 = (f32[2,768,256]{2,1,0:T(8,128)S(1)}, f32[2,768,256]{2,1,0:T(8,128)}, u32[]{:S(2)}) copy-start(f32[2,768,256]{2,1,0:T(8,128)} %copy-done.6) | copy-start | bytes 4718596
  53.3 16.7 %collective-permute-start.18 = (f32[32,2048]{1,0:T(8,128)S(1)}, f32[32,2048]{1,0:T(8,128)S(1)}, u32[]{:S(2)}, u32[]{:S(2)}) collective-permute-start(f32[32,2048]{1,0:T(8,128)S(1)} %get-tuple-element.69), channel_id=1, source_target_pairs={{0,96},{16,112},{32,0},{48,16},{64,32},{80,48},{96,64},{112,80},{1... | collective-permute-start | bytes 786440 | tf_op jit(solution)/shard_map/ppermute | solution.py:286
  56.3 13.6 %collective-permute-start.17 = (f32[32,2048]{1,0:T(8,128)S(1)}, f32[32,2048]{1,0:T(8,128)S(1)}, u32[]{:S(2)}, u32[]{:S(2)}) collective-permute-start(f32[32,2048]{1,0:T(8,128)S(1)} %get-tuple-element.59.refs_4_), channel_id=1, source_target_pairs={{0,32},{16,48},{32,64},{48,80},{64,96},{80,112},{96,0},{112,16},{1... | collective-permute-start | bytes 786440 | tf_op jit(solution)/shard_map/ppermute | solution.py:286
  56.8 12.0 %collective-permute-start.9 = (f32[192,256]{1,0:T(8,128)S(1)}, f32[192,256]{1,0:T(8,128)S(1)}, u32[]{:S(2)}, u32[]{:S(2)}) collective-permute-start(f32[192,256]{1,0:T(8,128)S(1)} %get-tuple-element.61), channel_id=1, source_target_pairs={{0,4},{1,5},{2,6},{3,7},{4,8},{5,9},{6,10},{7,11},{8,12},{9,13},{1... | collective-permute-start | bytes 589832 | tf_op jit(solution)/shard_map/ppermute | solution.py:294
  58.7 10.1 %collective-permute-start.10 = (f32[192,256]{1,0:T(8,128)S(1)}, f32[192,256]{1,0:T(8,128)S(1)}, u32[]{:S(2)}, u32[]{:S(2)}) collective-permute-start(f32[192,256]{1,0:T(8,128)S(1)} %get-tuple-element.62), channel_id=1, source_target_pairs={{0,12},{1,13},{2,14},{3,15},{4,0},{5,1},{6,2},{7,3},{8,4},{9,5},{1... | collective-permute-start | bytes 589832 | tf_op jit(solution)/shard_map/ppermute | solution.py:294
  60.1 9.8 %collective-permute-start.11 = (f32[192,256]{1,0:T(8,128)S(1)}, f32[192,256]{1,0:T(8,128)S(1)}, u32[]{:S(2)}, u32[]{:S(2)}) collective-permute-start(f32[192,256]{1,0:T(8,128)S(1)} %get-tuple-element.63), channel_id=1, source_target_pairs={{0,8},{1,9},{2,10},{3,11},{4,12},{5,13},{6,14},{7,15},{8,0},{9,1},... | collective-permute-start | bytes 589832 | tf_op jit(solution)/shard_map/ppermute | solution.py:294
  70.1 20.1 %collective-permute-start.19 = (f32[96,2048]{1,0:T(8,128)S(1)}, f32[96,2048]{1,0:T(8,128)S(1)}, u32[]{:S(2)}, u32[]{:S(2)}) collective-permute-start(f32[96,2048]{1,0:T(8,128)S(1)} %get-tuple-element.70), channel_id=1, source_target_pairs={{0,32},{16,48},{32,64},{48,80},{64,96},{80,112},{96,0},{112,16},{1... | collective-permute-start | bytes 2359304 | tf_op jit(solution)/shard_map/ppermute | solution.py:286
  70.5 19.8 %collective-permute-start.20 = (f32[96,2048]{1,0:T(8,128)S(1)}, f32[96,2048]{1,0:T(8,128)S(1)}, u32[]{:S(2)}, u32[]{:S(2)}) collective-permute-start(f32[96,2048]{1,0:T(8,128)S(1)} %get-tuple-element.71), channel_id=1, source_target_pairs={{0,96},{16,112},{32,0},{48,16},{64,32},{80,48},{96,64},{112,80},{1... | collective-permute-start | bytes 2359304 | tf_op jit(solution)/shard_map/ppermute | solution.py:286
  73.4 5.7 %collective-permute-start.12 = (f32[192,256]{1,0:T(8,128)S(1)}, f32[192,256]{1,0:T(8,128)S(1)}, u32[]{:S(2)}, u32[]{:S(2)}) collective-permute-start(f32[192,256]{1,0:T(8,128)S(1)} %shard_map.87.refs_0_.refs_6_), channel_id=1, source_target_pairs={{0,1},{1,0},{2,3},{3,2},{4,5},{5,4},{6,7},{7,6},{8,9},{9,8},{10,11... | collective-permute-start | bytes 589832 | tf_op jit(solution)/shard_map/ppermute | solution.py:290
  79.1 7.7 %collective-permute-start.13 = (f32[192,256]{1,0:T(8,128)S(1)}, f32[192,256]{1,0:T(8,128)S(1)}, u32[]{:S(2)}, u32[]{:S(2)}) collective-permute-start(f32[192,256]{1,0:T(8,128)S(1)} %shard_map.88.refs_1_), channel_id=1, source_target_pairs={{0,2},{1,3},{2,0},{3,1},{4,6},{5,7},{6,4},{7,5},{8,10},{9,11},{10,... | collective-permute-start | bytes 589832 | tf_op jit(solution)/shard_map/ppermute | solution.py:290
  90.4 18.9 %collective-permute-start.23 = (f32[64,2048]{1,0:T(8,128)S(1)}, f32[64,2048]{1,0:T(8,128)S(1)}, u32[]{:S(2)}, u32[]{:S(2)}) collective-permute-start(f32[64,2048]{1,0:T(8,128)S(1)} %get-tuple-element.78), channel_id=1, source_target_pairs={{0,96},{16,112},{32,0},{48,16},{64,32},{80,48},{96,64},{112,80},{1... | collective-permute-start | bytes 1572872 | tf_op jit(solution)/shard_map/ppermute | solution.py:286
  93.4 15.9 %collective-permute-start.22 = (f32[64,2048]{1,0:T(8,128)S(1)}, f32[64,2048]{1,0:T(8,128)S(1)}, u32[]{:S(2)}, u32[]{:S(2)}) collective-permute-start(f32[64,2048]{1,0:T(8,128)S(1)} %get-tuple-element.74.refs_3_), channel_id=1, source_target_pairs={{0,32},{16,48},{32,64},{48,80},{64,96},{80,112},{96,0},{112,16},{1... | collective-permute-start | bytes 1572872 | tf_op jit(solution)/shard_map/ppermute | solution.py:286
  93.5 15.8 %collective-permute-start.21 = (f32[32,2048]{1,0:T(8,128)S(1)}, f32[32,2048]{1,0:T(8,128)S(1)}, u32[]{:S(2)}, u32[]{:S(2)}) collective-permute-start(f32[32,2048]{1,0:T(8,128)S(1)} %get-tuple-element.76), channel_id=1, source_target_pairs={{0,128},{16,144},{32,160},{48,176},{64,192},{80,208},{96,224},{112... | collective-permute-start | bytes 786440 | tf_op jit(solution)/shard_map/ppermute | solution.py:286
  98.1 18.0 %collective-permute-start.16 = (f32[192,256]{1,0:T(8,128)S(1)}, f32[192,256]{1,0:T(8,128)S(1)}, u32[]{:S(2)}, u32[]{:S(2)}) collective-permute-start(f32[192,256]{1,0:T(8,128)S(1)} %shard_map.89.refs_1_.refs_4_), channel_id=1, source_target_pairs={{0,8},{1,9},{2,10},{3,11},{4,12},{5,13},{6,14},{7,15},{8,0},{9,1},... | collective-permute-start | bytes 589832 | tf_op jit(solution)/shard_map/ppermute | solution.py:294
  109.4 17.2 %collective-permute-start.26 = (f32[16,4096]{1,0:T(8,128)S(1)}, f32[16,4096]{1,0:T(8,128)S(1)}, u32[]{:S(2)}, u32[]{:S(2)}) collective-permute-start(f32[16,4096]{1,0:T(8,128)S(1)} %get-tuple-element.83), channel_id=1, source_target_pairs={{0,16},{16,0},{32,48},{48,32},{64,80},{80,64},{96,112},{112,96},{1... | collective-permute-start | bytes 786440 | tf_op jit(solution)/shard_map/ppermute | solution.py:286
  109.5 7.3 %collective-permute-start.15 = (f32[192,256]{1,0:T(8,128)S(1)}, f32[192,256]{1,0:T(8,128)S(1)}, u32[]{:S(2)}, u32[]{:S(2)}) collective-permute-start(f32[192,256]{1,0:T(8,128)S(1)} %shard_map.89.refs_1_.refs_4_), channel_id=1, source_target_pairs={{0,12},{1,13},{2,14},{3,15},{4,0},{5,1},{6,2},{7,3},{8,4},{9,5},{1... | collective-permute-start | bytes 589832 | tf_op jit(solution)/shard_map/ppermute | solution.py:294
  111.3 8.2 %collective-permute-start.14 = (f32[192,256]{1,0:T(8,128)S(1)}, f32[192,256]{1,0:T(8,128)S(1)}, u32[]{:S(2)}, u32[]{:S(2)}) collective-permute-start(f32[192,256]{1,0:T(8,128)S(1)} %shard_map.89.refs_1_.refs_4_), channel_id=1, source_target_pairs={{0,4},{1,5},{2,6},{3,7},{4,8},{5,9},{6,10},{7,11},{8,12},{9,13},{1... | collective-permute-start | bytes 589832 | tf_op jit(solution)/shard_map/ppermute | solution.py:294
  111.6 12.0 %collective-permute-start.24 = (f32[16,2048]{1,0:T(8,128)S(1)}, f32[16,2048]{1,0:T(8,128)S(1)}, u32[]{:S(2)}, u32[]{:S(2)}) collective-permute-start(f32[16,2048]{1,0:T(8,128)S(1)} %get-tuple-element.81), channel_id=1, source_target_pairs={{0,128},{16,144},{32,160},{48,176},{64,192},{80,208},{96,224},{112... | collective-permute-start | bytes 393224 | tf_op jit(solution)/shard_map/ppermute | solution.py:286
  116.0 10.6 %collective-permute-start.25 = (f32[16,2048]{1,0:T(8,128)S(1)}, f32[16,2048]{1,0:T(8,128)S(1)}, u32[]{:S(2)}, u32[]{:S(2)}) collective-permute-start(f32[16,2048]{1,0:T(8,128)S(1)} %get-tuple-element.82), channel_id=1, source_target_pairs={{0,144},{16,128},{32,176},{48,160},{64,208},{80,192},{96,240},{112... | collective-permute-start | bytes 393224 | tf_op jit(solution)/shard_map/ppermute | solution.py:286
